TPU v7x, 32 devices: a whole 2x2x4 slice. The times are simulated.
32 devices in a mesh: sec: 2 (over x), grp: 16 (over z, y, core), tp: 1.
Axes of the slice: x: 2, y: 2, z: 4, core: 2. Of those that a mesh axis runs over, the one named last changes fastest.
Arguments:
- hidden_in: bfloat16 [128, 7168], P(('sec', 'grp', 'tp')), may hold values from -6 to 6
- queries: bfloat16 [128, 128, 1, 576], P(('sec', 'grp'), None, 'tp'), may hold values from -61 to 61
- latent_cache: bfloat16 [128, 64, 576], P(('sec', 'grp')), may hold values from -6 to 6
- lengths: int32 [128], P(('sec', 'grp')), may hold values from 2 to 64, as said below
- w_uv: bfloat16 [128, 1, 512, 128], P(None, 'tp'), may hold values from -0.75 to 0.75
- attn_weight: bfloat16 [128, 1, 128, 7168], P(None, 'tp', None, 'grp'), may hold values from -0.046875 to 0.046875
- norm_gain: float32 [7168], replicated, may hold values from 0.1 to 1.9
- router: bfloat16 [7168, 32], replicated, may hold values from -0.0625 to 0.0625
- routes: int32 [128, 8], P(('sec', 'grp', 'tp')), may hold values from 0 to 31, all different within a row; in each aligned block of 4 rows (0 to 3, 4 to 7, ...) at most 2 rows name the same one
- live_counts: int32 [32], P(('sec', 'grp', 'tp')), may hold values from 3 to 4, as said below
- expert_in: bfloat16 [32, 7168, 2, 1024], P(('sec', 'grp'), None, None, 'tp'), may hold values from -0.0625 to 0.0625
- expert_out: bfloat16 [32, 1024, 7168], P(('sec', 'grp'), 'tp'), may hold values from -0.5 to 0.5
Outputs:
- layer_out: bfloat16 [128, 7168], P(('sec', 'grp', 'tp'))
Inputs may be any that keep to these rules, and one draw needn't show every extreme that they name: `lengths`: some request has exactly 64 cached positions and some has 2. `live_counts`: some device has all 4 slots live and some has exactly 3. `routes`: the 8 experts of a token differ. Within the rows of one device (aligned blocks of 4 rows) no expert is named by more than 2 rows, a bound that some block reaches.
All inputs are finite; a program needn't handle non-finite values.
Results may differ from a plain program's by a relative error of at most 0.018.
Values may be sent and summed in bfloat16 or wider, within the bound.
A program may use at most 192 MiB of HBM per device.

v0:
```python
import jax
import jax.numpy as jnp
from jax import lax
from jax.sharding import PartitionSpec as P

score_scale = 192.0 ** (-0.5)
route_scale = 2.5


def expert_slice(rows_in, expert_in, expert_out):
    width = rows_in.shape[1]
    slice_width = expert_in.shape[3]
    gate_up = jnp.dot(
        rows_in, expert_in[0].reshape(width, 2 * slice_width), preferred_element_type=jnp.float32
    )
    activated = (jax.nn.silu(gate_up[:, :slice_width]) * gate_up[:, slice_width:]).astype(
        jnp.bfloat16
    )
    return jnp.dot(activated, expert_out[0], preferred_element_type=jnp.float32).astype(
        jnp.bfloat16
    )


def shards(
    hidden_in,
    queries,
    latent_cache,
    lengths,
    w_uv,
    attn_weight,
    norm_gain,
    router,
    routes,
    live_counts,
    expert_in,
    expert_out,
):
    count_of_tokens, width = hidden_in.shape
    sections = lax.axis_size("sec")
    expert_groups = lax.axis_size("grp")
    slices = lax.axis_size("tp")
    latent_width = w_uv.shape[2]
    query_block = queries[:, :, 0, :]
    scores = (
        jnp.einsum("bhr,bpr->bhp", query_block, latent_cache, preferred_element_type=jnp.float32)
        * score_scale
    )
    positions = jnp.arange(latent_cache.shape[1])
    visible = positions[None, None, :] < lengths[:, None, None]
    scores = jnp.where(visible, scores, -1e30)
    highest = jnp.max(scores, axis=2, keepdims=True)
    raised = jnp.exp(scores - highest)
    softmax_weights = (raised / jnp.sum(raised, axis=2, keepdims=True)).astype(jnp.bfloat16)
    latent_out = jnp.einsum(
        "bhp,bpc->bhc",
        softmax_weights,
        latent_cache[:, :, :latent_width],
        preferred_element_type=jnp.float32,
    ).astype(jnp.bfloat16)
    head_out = jnp.einsum(
        "bhc,hcv->bhv", latent_out, w_uv[:, 0], preferred_element_type=jnp.float32
    ).astype(jnp.bfloat16)
    head_rows = head_out.reshape(head_out.shape[0], -1)
    out_block = attn_weight[:, 0].reshape(-1, attn_weight.shape[3])
    partial_value = jnp.dot(
        lax.all_gather(head_rows, "grp", axis=0, tiled=True),
        out_block,
        preferred_element_type=jnp.float32,
    )
    partial_value = partial_value.reshape(
        expert_groups, slices, count_of_tokens, partial_value.shape[1]
    )
    summed = lax.psum_scatter(
        partial_value.astype(jnp.bfloat16), "tp", scatter_dimension=1, tiled=True
    ).astype(jnp.float32)
    column_part = summed[:, 0].astype(jnp.bfloat16)
    attention = lax.all_to_all(column_part, "grp", split_axis=0, concat_axis=2, tiled=True)[0]
    residual = hidden_in.astype(jnp.float32) + attention.astype(jnp.float32)
    normalized_input = (
        residual
        * lax.rsqrt(jnp.mean(residual * residual, axis=1, keepdims=True) + 1e-06)
        * norm_gain
    ).astype(jnp.bfloat16)
    experts = router.shape[1]
    per_token = routes.shape[1]
    capacity = max(2, 2 * count_of_tokens * per_token // experts)
    affinity = jax.nn.sigmoid(jnp.dot(normalized_input, router, preferred_element_type=jnp.float32))
    picked = routes[:, :, None] == jnp.arange(experts)[None, None, :]
    chosen = jnp.sum(jnp.where(picked, affinity[:, None, :], 0.0), axis=2)
    living = jnp.arange(count_of_tokens) < live_counts[0]
    gate_weights = (
        route_scale
        * chosen
        / jnp.sum(chosen, axis=1, keepdims=True)
        * living[:, None].astype(jnp.float32)
    )
    routed = jnp.any(picked, axis=1) & living[:, None]
    routed_count = routed.astype(jnp.int32)
    slot_index = jnp.cumsum(routed_count, axis=0) - routed_count
    placed_tokens = routed[:, :, None] & (
        slot_index[:, :, None] == jnp.arange(capacity)[None, None, :]
    )
    expert_gate = jnp.sum(jnp.where(picked, gate_weights[:, :, None], 0.0), axis=1)
    outgoing = jnp.einsum(
        "poy,pj->oyj",
        placed_tokens.astype(jnp.bfloat16),
        normalized_input,
        preferred_element_type=jnp.float32,
    ).astype(jnp.bfloat16)
    combine_rows = (placed_tokens.astype(jnp.float32) * expert_gate[:, :, None]).reshape(
        count_of_tokens, experts * capacity
    )
    once_rows = outgoing.reshape(sections, expert_groups, capacity, width)
    arrived = lax.all_to_all(
        lax.all_to_all(once_rows, "sec", split_axis=0, concat_axis=0, tiled=True),
        "grp",
        split_axis=1,
        concat_axis=1,
        tiled=True,
    )
    local_rows = arrived.reshape(-1, width)
    every_out = expert_slice(
        lax.all_gather(local_rows, "tp", axis=0, tiled=True), expert_in, expert_out
    )
    own_sums = lax.psum_scatter(
        every_out.astype(jnp.float32).astype(jnp.bfloat16), "tp", scatter_dimension=0, tiled=True
    ).astype(jnp.float32)
    own_sums = own_sums.reshape(sections, expert_groups, capacity, width)
    back_rows = lax.all_to_all(
        lax.all_to_all(
            own_sums.astype(jnp.bfloat16), "grp", split_axis=1, concat_axis=1, tiled=True
        ),
        "sec",
        split_axis=0,
        concat_axis=0,
        tiled=True,
    ).astype(own_sums.dtype)
    expert_sums = back_rows.reshape(experts * capacity, width)
    expert_mix = jnp.dot(combine_rows, expert_sums, precision=lax.Precision.HIGHEST)
    return (residual + expert_mix).astype(jnp.bfloat16)


def solution(mesh):
    placed = (
        P(("sec", "grp", "tp"), None),
        P(("sec", "grp"), None, "tp", None),
        P(("sec", "grp"), None, None),
        P(("sec", "grp")),
        P(None, "tp", None, None),
        P(None, "tp", None, "grp"),
        P(),
        P(),
        P(("sec", "grp", "tp"), None),
        P(("sec", "grp", "tp")),
        P(("sec", "grp"), None, None, "tp"),
        P(("sec", "grp"), "tp", None),
    )
    return jax.shard_map(
        shards, mesh=mesh, in_specs=placed, out_specs=P(("sec", "grp", "tp"), None), check_vma=False
    )
```

profile of v0, /device:TPU:0, one launch (start us, length us, event | category | flops | bytes accessed | tf_op | source)
XLA Modules:
  0.0 206.6 jit_solution(17635677142318502580)
XLA Ops:
  6.5 0.8 iota_compare_fusion.1
  7.6 1.2 fusion.18
  8.9 1.3 convolution_convert_fusion.1
  10.2 7.7 %fusion.15 = bf16[1,4,16384]{2,1,0:T(4,128)(2,1)} fusion(bf16[128,1,512,128]{3,2,1,0:T(8,128)(2,1)} %param.16, bf16[4,128,512]{2,1,0:T(8,128)(2,1)S(1)} %convolution_convert_fusion.1), kind=kOutput, calls=%fused_computation.14 | convolution fusion | flops 67174400 | bytes 17432576 | tf_op jit(solution)/shard_map/bhc,hcv->bhv/dot_general | solution.py:60
  17.9 16.6 %copy.48 = bf16[128,1,128,448]{2,0,3,1:T(8,128)(2,1)} copy(bf16[128,1,128,448]{2,3,1,0:T(8,128)(2,1)} %param.17) | data formatting | bytes 29360128 | tf_op args[5]
  34.6 22.4 %reshape.210 = bf16[16384,448,1]{0,1,2:T(8,128)(2,1)} reshape(bf16[128,1,128,448]{2,0,3,1:T(8,128)(2,1)} %copy.48) | data formatting | bytes 29360128 | tf_op jit(solution)/shard_map/reshape;squeeze | solution.py:64
  57.9 4.3 %all-gather.3.cloned.1.call-done = bf16[16,4,16384]{2,1,0:T(4,128)(2,1)} async-done(((bf16[1,4,16384]{2,1,0:T(4,128)(2,1)}), bf16[16,4,16384]{2,1,0:T(4,128)(2,1)}) %all-gather.3.cloned.1.call-update) | async-done | bytes 2097168 | tf_op jit(solution)/shard_map/all_gather | solution.py:66
  62.2 10.2 %fusion.20 = bf16[16,4,448]{2,0,1:T(8,128)(2,1)S(1)} fusion(bf16[16384,448,1]{0,1,2:T(8,128)(2,1)} %reshape.210, bf16[16,4,16384]{2,1,0:T(4,128)(2,1)} %all-gather.3.cloned.1.call-done), kind=kOutput, calls=%fused_computation.18 | convolution fusion | flops 939552768 | bytes 16834560 | tf_op jit(solution)/shard_map/dot_general | solution.py:65
  73.0 3.5 %all-to-all-start = ((bf16[16,4,448]{2,1,0:T(4,128)(2,1)}), bf16[16,4,448]{2,1,0:T(4,128)(2,1)S(1)}, u32[]{:S(2)}, u32[]{:S(2)}) async-start(bf16[16,4,448]{2,1,0:T(4,128)(2,1)} %copy.50), calls=%async_computation | async-start | bytes 131072 | tf_op jit(solution)/shard_map/all_to_all | solution.py:77
  76.7 6.7 %all-to-all-done = bf16[16,4,448]{2,1,0:T(4,128)(2,1)S(1)} async-done(((bf16[16,4,448]{2,1,0:T(4,128)(2,1)}), bf16[16,4,448]{2,1,0:T(4,128)(2,1)S(1)}, u32[]{:S(2)}, u32[]{:S(2)}) %all-to-all-start) | async-done | bytes 57376 | tf_op jit(solution)/shard_map/all_to_all | solution.py:77
  85.0 0.9 copy.56
  86.0 14.6 %all_to_all.29 = bf16[2,16,2,7168]{3,2,1,0:T(2,128)(2,1)S(1)} all-to-all(bf16[2,16,2,7168]{3,2,1,0:T(2,128)(2,1)S(1)} %copy.56), channel_id=1, replica_groups=mesh['sec'=2,'grp'=16,'tp'=1] {'sec'}, dimensions={0} | all-to-all | bytes 1835008 | tf_op jit(solution)/shard_map/all_to_all | solution.py:115
  100.6 1.6 copy.57
  102.2 4.5 %all-to-all-start.2 = ((bf16[2,16,2,7168]{3,2,0,1:T(2,128)(2,1)}), bf16[2,16,2,7168]{3,2,0,1:T(2,128)(2,1)}, u32[]{:S(2)}, u32[]{:S(2)}) async-start(bf16[2,16,2,7168]{3,2,0,1:T(2,128)(2,1)} %copy.57), calls=%async_computation.2 | async-start | bytes 1835008 | tf_op jit(solution)/shard_map/all_to_all | solution.py:114
  106.7 20.0 %copy.61 = bf16[896,8,2,1024]{3,1,2,0:T(8,128)(2,1)} copy(bf16[896,8,2,1024]{3,2,1,0:T(2,128)(2,1)} %bitcast.51) | data formatting | bytes 58720256
  127.3 2.9 %copy.58 = bf16[2,16,2,7168]{3,2,1,0:T(2,128)(2,1)} copy(bf16[2,16,2,7168]{3,2,0,1:T(2,128)(2,1)} %all-to-all-done.2) | data formatting | bytes 1835008 | tf_op jit(solution)/shard_map/all_to_all | solution.py:114
  130.2 3.2 %reshape.202 = bf16[64,7168]{1,0:T(8,128)(2,1)} reshape(bf16[2,16,2,7168]{3,2,1,0:T(2,128)(2,1)} %copy.58) | data formatting | bytes 1835008 | tf_op jit(solution)/shard_map/reshape | solution.py:121
  133.4 12.4 %fusion.41 = f32[64,2048]{1,0:T(8,128)S(1)} fusion(bf16[64,7168]{1,0:T(8,128)(2,1)} %reshape.202, bf16[7168,2048]{1,0:T(8,128)(2,1)} %bitcast.50), kind=kOutput, calls=%fused_computation.55 | convolution fusion | flops 1879048192 | bytes 30801920 | tf_op jit(solution)/shard_map/dot_general | solution.py:13
  145.9 0.8 slice-done.3
  146.7 3.6 %fusion.5 = bf16[64,7168]{1,0:T(8,128)(2,1)} fusion(bf16[1,1024,7168]{2,1,0:T(8,128)(2,1)S(1)} %bitcast.53, f32[64,2048]{1,0:T(8,128)S(1)} %fusion.41), kind=kOutput, calls=%fused_computation.6 | convolution fusion | flops 940376064 | bytes 16121856 | tf_op jit(solution)/shard_map/dot_general | solution.py:19
  150.3 2.3 %convert_element_type.94 = bf16[2,16,2,7168]{3,2,1,0:T(2,128)(2,1)S(1)} reshape(bf16[64,7168]{1,0:T(8,128)(2,1)} %fusion.5) | data formatting | bytes 1835008 | tf_op jit(solution)/shard_map/convert_element_type | solution.py:131
  153.3 28.5 %all_to_all.30 = bf16[2,16,2,7168]{3,2,0,1:T(2,128)(2,1)S(1)} all-to-all(bf16[2,16,2,7168]{3,2,0,1:T(2,128)(2,1)S(1)} %copy.59), channel_id=1, replica_groups=mesh['sec'=2,'grp'=16,'tp'=1] {'grp'}, dimensions={1} | all-to-all | bytes 1835008 | tf_op jit(solution)/shard_map/all_to_all | solution.py:130
  182.4 15.8 %all_to_all.31 = bf16[2,16,2,7168]{3,2,1,0:T(2,128)(2,1)S(1)} all-to-all(bf16[2,16,2,7168]{3,2,1,0:T(2,128)(2,1)S(1)} %copy.60), channel_id=1, replica_groups=mesh['sec'=2,'grp'=16,'tp'=1] {'sec'}, dimensions={0} | all-to-all | bytes 1835008 | tf_op jit(solution)/shard_map/all_to_all | solution.py:129
  198.6 1.2 fusion.8
  (48 shorter events, 5.3 us)
Async XLA Ops:
  6.5 1.1 copy-start
  6.5 55.6 %all-gather.3.cloned.1.call-start = ((), (), s32[]{:S(2)}) async-start(), calls=%async_computation.5 | async-start | bytes 2228224 | tf_op jit(solution)/shard_map/all_gather | solution.py:66
  34.6 23.1 %copy-start.4 = (s32[4,8]{1,0:T(4,128)S(1)}, s32[4,8]{1,0:T(4,128)}, u32[]{:S(2)}) copy-start(s32[4,8]{1,0:T(4,128)} %param.20) | copy-start | bytes 388
  56.9 26.7 %copy-start.2 = (bf16[4,7168]{1,0:T(4,128)(2,1)S(1)}, bf16[4,7168]{1,0:T(4,128)(2,1)}, u32[]{:S(2)}) copy-start(bf16[4,7168]{1,0:T(4,128)(2,1)} %param.12) | copy-start | bytes 172036
  56.9 26.9 %copy-start.3 = (f32[7168]{0:T(1024)S(1)}, f32[7168]{0:T(1024)}, u32[]{:S(2)}) copy-start(f32[7168]{0:T(1024)} %param.18) | copy-start | bytes 86020
  56.9 27.0 %copy-start.5 = (bf16[7168,32]{0,1:T(8,128)(2,1)S(1)}, bf16[7168,32]{0,1:T(8,128)(2,1)}, u32[]{:S(2)}) copy-start(bf16[7168,32]{0,1:T(8,128)(2,1)} %param.19) | copy-start | bytes 1376260
  73.0 10.4 %all-to-all-start = ((bf16[16,4,448]{2,1,0:T(4,128)(2,1)}), bf16[16,4,448]{2,1,0:T(4,128)(2,1)S(1)}, u32[]{:S(2)}, u32[]{:S(2)}) async-start(bf16[16,4,448]{2,1,0:T(4,128)(2,1)} %copy.50), calls=%async_computation | async-start | bytes 131072 | tf_op jit(solution)/shard_map/all_to_all | solution.py:77
  102.2 25.1 %all-to-all-start.2 = ((bf16[2,16,2,7168]{3,2,0,1:T(2,128)(2,1)}), bf16[2,16,2,7168]{3,2,0,1:T(2,128)(2,1)}, u32[]{:S(2)}, u32[]{:S(2)}) async-start(bf16[2,16,2,7168]{3,2,0,1:T(2,128)(2,1)} %copy.57), calls=%async_computation.2 | async-start | bytes 1835008 | tf_op jit(solution)/shard_map/all_to_all | solution.py:114
  127.3 18.6 %slice-start = ((s8[14680064]{0:T(1024)(128)(4,1)}), s8[2097152]{0:T(1024)(128)(4,1)S(1)}, s32[]{:S(2)}) async-start(s8[14680064]{0:T(1024)(128)(4,1)} %bitcast.52), calls=%async_computation.6 | async-start | bytes 4194304
  133.4 12.5 %slice-start.1 = ((s8[14680064]{0:T(1024)(128)(4,1)}), s8[4194304]{0:T(1024)(128)(4,1)S(1)}, s32[]{:S(2)}) async-start(s8[14680064]{0:T(1024)(128)(4,1)} %bitcast.52), calls=%async_computation.7 | async-start | bytes 8388608
  133.4 12.5 %slice-start.2 = ((s8[14680064]{0:T(1024)(128)(4,1)}), s8[4194304]{0:T(1024)(128)(4,1)S(1)}, s32[]{:S(2)}) async-start(s8[14680064]{0:T(1024)(128)(4,1)} %bitcast.52), calls=%async_computation.8 | async-start | bytes 8388608
  133.4 13.3 %slice-start.3 = ((s8[14680064]{0:T(1024)(128)(4,1)}), s8[4194304]{0:T(1024)(128)(4,1)S(1)}, s32[]{:S(2)}) async-start(s8[14680064]{0:T(1024)(128)(4,1)} %bitcast.52), calls=%async_computation.9 | async-start | bytes 8388608
  133.4 66.3 %copy-start.1 = (bf16[4,128,1,576]{1,3,2,0:T(8,128)(2,1)S(1)}, bf16[4,128,1,576]{1,3,2,0:T(8,128)(2,1)}, u32[]{:S(2)}) copy-start(bf16[4,128,1,576]{1,3,2,0:T(8,128)(2,1)} %param.13) | copy-start | bytes 1769476
Sparse Core Ops, SparseCore 0:
  18.0 44.0 all-gather.2
where the time goes:
time: 208 us; the launch traced here: 207 us
  local copies, waits for them, and re-layouts  73.8 us (35%)
  blocking collectives  59 us (28%)
  matrix products  38.2 us (18%)
  between operations  14.3 us (7%)
  waiting for transfers between devices  11.6 us (6%)
  starting transfers between devices  7.99 us (4%)
    unnamed x22, local copies, waits for them, and re-layouts  37.8 us
    all_to_all x1, blocking collectives, shards(): lax.all_to_all(own_sums.astype(jnp.bfloat16), 'grp', split_axis=1, concat...  28.5 us
    another operation x1, local copies, waits for them, and re-layouts, shards(): out_block = attn_weight[:, 0].reshape(-1, attn_weight.shape[3])  22.4 us
    all_to_all x1, blocking collectives, shards(): lax.all_to_all(lax.all_to_all(own_sums.astype(jnp.bfloat16), 'grp', split...  15.8 us
    all_to_all x1, blocking collectives, shards(): lax.all_to_all(once_rows, 'sec', split_axis=0, concat_axis=0, tiled=True)  14.6 us
    dot_general x1, matrix products, expert_slice(): jnp.dot(rows_in, expert_in[0].reshape(width, 2 * slice_width), preferred_...  12.4 us
    dot_general x1, matrix products, shards(): jnp.dot(lax.all_gather(head_rows, 'grp', axis=0, tiled=True), out_block,...  10.2 us
    dot_general x1, matrix products, shards(): jnp.einsum('bhc,hcv->bhv', latent_out, w_uv[:, 0], preferred_element_type...  7.68 us
  transfers between devices with their start and end apart: 3, of which 3 were waited for; matrix products, arithmetic and copies ran while one was open for 29% of the time, Pallas kernels for 0%

commit v1 on v0

v1 whole, which is shorter than its diff:
```python
import functools

import jax
import jax.numpy as jnp
from jax import lax
from jax.experimental import pallas as pl
from jax.experimental.pallas import tpu as pltpu
from jax.sharding import PartitionSpec as P

score_scale = 192.0 ** (-0.5)
route_scale = 2.5


def divisor_at_most(number, most):
    return max(d for d in range(1, most + 1) if number % d == 0)


def project_kernel(heads_step, x_ref, w_ref, out_ref, total):
    step = pl.program_id(0)

    @pl.when(step == 0)
    def _():
        total[...] = jnp.zeros_like(total)

    value_width = w_ref.shape[2]
    part = jnp.zeros(total.shape, jnp.float32)
    pair = 2 if heads_step % 2 == 0 else 1
    for i in range(0, heads_step, pair):
        block = jnp.concatenate([w_ref[i + k] for k in range(pair)], axis=1)
        part += lax.dot_general(
            x_ref[:, i * value_width : (i + pair) * value_width],
            block,
            (((1,), (1,)), ((), ())),
            preferred_element_type=jnp.float32,
        )
    total[...] += part

    @pl.when(step == pl.num_programs(0) - 1)
    def _():
        out_ref[...] = total[...].astype(out_ref.dtype)


def project(rows, weight):
    heads, columns, value_width = weight.shape
    tokens = rows.shape[0]
    heads_step = divisor_at_most(heads, 8)
    return pl.pallas_call(
        functools.partial(project_kernel, heads_step),
        grid=(heads // heads_step,),
        in_specs=[
            pl.BlockSpec((tokens, heads_step * value_width), lambda i: (0, i)),
            pl.BlockSpec((heads_step, columns, value_width), lambda i: (i, 0, 0)),
        ],
        out_specs=pl.BlockSpec((tokens, columns), lambda i: (0, 0)),
        out_shape=jax.ShapeDtypeStruct((tokens, columns), jnp.float32),
        scratch_shapes=[pltpu.VMEM((tokens, columns), jnp.float32)],
        compiler_params=pltpu.CompilerParams(vmem_limit_bytes=16 * 1024 * 1024),
        cost_estimate=pl.CostEstimate(
            flops=2 * tokens * heads * value_width * columns,
            bytes_accessed=2 * heads * value_width * (columns + tokens),
            transcendentals=0,
        ),
        name="project",
    )(rows, weight)


def shards(
    hidden_in,
    queries,
    latent_cache,
    lengths,
    w_uv,
    attn_weight,
    norm_gain,
    router,
    routes,
    live_counts,
    expert_in,
    expert_out,
):
    everyone = ("sec", "grp", "tp")
    own_tokens, width = hidden_in.shape
    sections = lax.axis_size("sec")
    expert_groups = lax.axis_size("grp")
    latent_width = w_uv.shape[2]
    experts = router.shape[1]

    picked = jnp.any(routes[:, :, None] == jnp.arange(experts)[None, None, :], axis=1)
    living = jnp.arange(own_tokens) < live_counts[0]
    chosen_mask = (picked & living[:, None]).astype(jnp.float32)
    mask_all = lax.all_gather(chosen_mask, everyone, axis=0, tiled=True)
    hidden_all = lax.all_gather(hidden_in, everyone, axis=0, tiled=True)

    query_block = queries[:, :, 0, :]
    scores = (
        jnp.einsum("bhr,bpr->bhp", query_block, latent_cache, preferred_element_type=jnp.float32)
        * score_scale
    )
    positions = jnp.arange(latent_cache.shape[1])
    visible = positions[None, None, :] < lengths[:, None, None]
    scores = jnp.where(visible, scores, -1e30)
    highest = jnp.max(scores, axis=2, keepdims=True)
    raised = jnp.exp(scores - highest)
    softmax_weights = (raised / jnp.sum(raised, axis=2, keepdims=True)).astype(jnp.bfloat16)
    latent_out = jnp.einsum(
        "bhp,bpc->bhc",
        softmax_weights,
        latent_cache[:, :, :latent_width],
        preferred_element_type=jnp.float32,
    ).astype(jnp.bfloat16)
    head_out = jnp.einsum(
        "bhc,hcv->bhv", latent_out, w_uv[:, 0], preferred_element_type=jnp.float32
    ).astype(jnp.bfloat16)
    head_rows = head_out.reshape(head_out.shape[0], -1)
    group_rows = lax.all_gather(head_rows, "grp", axis=0, tiled=True)
    column_part = project(group_rows, jnp.transpose(attn_weight[:, 0], (0, 2, 1)))
    if lax.axis_size("tp") > 1:
        column_part = lax.psum(column_part, "tp")
    column_part = column_part.astype(jnp.bfloat16)
    gathered = lax.all_gather(column_part, ("sec", "grp"), axis=0, tiled=False)
    section_tokens, columns = column_part.shape
    attention = (
        gathered.reshape(sections, expert_groups, section_tokens, columns)
        .transpose(0, 2, 1, 3)
        .reshape(sections * section_tokens, width)
    )
    residual = hidden_all.astype(jnp.float32) + attention.astype(jnp.float32)
    normed = (
        residual
        * lax.rsqrt(jnp.mean(residual * residual, axis=1, keepdims=True) + 1e-06)
        * norm_gain
    ).astype(jnp.bfloat16)
    affinity = jax.nn.sigmoid(jnp.dot(normed, router, preferred_element_type=jnp.float32))
    chosen = affinity * mask_all
    live_all = jnp.max(mask_all, axis=1, keepdims=True) > 0.0
    gate_all = jnp.where(
        live_all, route_scale * chosen / jnp.sum(chosen, axis=1, keepdims=True), 0.0
    )
    group = lax.axis_index("sec") * expert_groups + lax.axis_index("grp")
    own_gate = jnp.sum(
        jnp.where(jnp.arange(experts)[None, :] == group, gate_all, 0.0), axis=1, keepdims=True
    )

    slice_width = expert_in.shape[3]
    gate_up = jnp.dot(
        normed, expert_in[0].reshape(width, 2 * slice_width), preferred_element_type=jnp.float32
    )
    activated = (jax.nn.silu(gate_up[:, :slice_width]) * gate_up[:, slice_width:]).astype(
        jnp.bfloat16
    )
    value = jnp.dot(activated, expert_out[0], preferred_element_type=jnp.float32)
    mixed = (value * own_gate).astype(jnp.bfloat16)
    expert_mix = lax.psum_scatter(mixed, everyone, scatter_dimension=0, tiled=True)
    place = group * lax.axis_size("tp") + lax.axis_index("tp")
    own_attention = lax.dynamic_slice_in_dim(attention, place * own_tokens, own_tokens, 0)
    own_residual = hidden_in.astype(jnp.float32) + own_attention.astype(jnp.float32)
    return (own_residual + expert_mix.astype(jnp.float32)).astype(jnp.bfloat16)


def solution(mesh):
    placed = (
        P(("sec", "grp", "tp"), None),
        P(("sec", "grp"), None, "tp", None),
        P(("sec", "grp"), None, None),
        P(("sec", "grp")),
        P(None, "tp", None, None),
        P(None, "tp", None, "grp"),
        P(),
        P(),
        P(("sec", "grp", "tp"), None),
        P(("sec", "grp", "tp")),
        P(("sec", "grp"), None, None, "tp"),
        P(("sec", "grp"), "tp", None),
    )
    return jax.shard_map(
        shards, mesh=mesh, in_specs=placed, out_specs=P(("sec", "grp", "tp"), None), check_vma=False
    )
```

time: 208 us -> 351 us (1.69)
  waiting for transfers between devices: 11.6 us -> 211 us
  local copies, waits for them, and re-layouts: 73.8 us -> 40.7 us
  blocking collectives: 59 us -> 39.9 us
  starting transfers between devices: 7.99 us -> 0.12 us
  Pallas kernels: 0 us -> 7.04 us
  matrix products: 38.2 us -> 31.2 us
  other arithmetic: 1.76 us -> 6.82 us
    unnamed x1 -> x5, waiting for transfers between devices: 0.02 us -> 133 us
    all_gather x1 -> x3, waiting for transfers between devices: 4.3 us -> 78.3 us  [the longest x1 43.5 us: shards(): group_rows = lax.all_gather(head_rows, 'grp', axis=0, tiled=True)]
    all_to_all x3 -> x0, blocking collectives: 59 us -> none  [the longest x1 28.5 us: shards(): lax.all_to_all(own_sums.astype(jnp.bfloat16), 'grp', split_axis=1, concat...]
    all_gather x0 -> x1, blocking collectives: none -> 39.9 us  [shards(): mask_all = lax.all_gather(chosen_mask, everyone, axis=0, tiled=True)]
    another operation x1 -> x0, local copies, waits for them, and re-layouts: 22.4 us -> none  [shards(): out_block = attn_weight[:, 0].reshape(-1, attn_weight.shape[3])]
    unnamed x22 -> x19, local copies, waits for them, and re-layouts: 37.8 us -> 28.5 us
    all_to_all x2 -> x0, starting transfers between devices: 7.99 us -> none  [the longest x1 4.49 us: shards(): lax.all_to_all(lax.all_to_all(once_rows, 'sec', split_axis=0, concat_axis...]
    all_to_all x2 -> x0, waiting for transfers between devices: 7.29 us -> none  [the longest x1 6.67 us: shards(): lax.all_to_all(column_part, 'grp', split_axis=0, concat_axis=2, tiled=True)]
  transfers between devices with their start and end apart: 3 -> 4, of which waited for: 3 -> 3; matrix products, arithmetic and copies ran while one was open for 29% -> 8% of each run, Pallas kernels for 0% -> 2%
where the time goes in v1:
time: 351 us
  waiting for transfers between devices  211 us (60%)
  local copies, waits for them, and re-layouts  40.7 us (12%)
  blocking collectives  39.9 us (11%)
  matrix products  31.2 us (9%)
  between operations  14 us (4%)
  Pallas kernels  7.04 us (2%)
  other arithmetic  6.82 us (2%)
    unnamed x5, waiting for transfers between devices  133 us
    all_gather x1, waiting for transfers between devices, shards(): group_rows = lax.all_gather(head_rows, 'grp', axis=0, tiled=True)  43.5 us
    all_gather x1, blocking collectives, shards(): mask_all = lax.all_gather(chosen_mask, everyone, axis=0, tiled=True)  39.9 us
    all_gather x1, waiting for transfers between devices, shards(): gathered = lax.all_gather(column_part, ('sec', 'grp'), axis=0, tiled=False)  34.9 us
    unnamed x19, local copies, waits for them, and re-layouts  28.5 us
    dot_general x1, matrix products, shards(): jnp.dot(normed, expert_in[0].reshape(width, 2 * slice_width), preferred_e...  11.6 us
    dot_general x1, matrix products, shards(): jnp.dot(activated, expert_out[0], preferred_element_type=jnp.float32)  8.62 us
    dot_general x1, matrix products, shards(): jnp.einsum('bhc,hcv->bhv', latent_out, w_uv[:, 0], preferred_element_type...  7.7 us
  transfers between devices with their start and end apart: 4, of which 3 were waited for; matrix products, arithmetic and copies ran while one was open for 8% of the time, Pallas kernels for 2%

profile of v1, /device:TPU:0, one launch (start us, length us, event | category | flops | bytes accessed | tf_op | source)
XLA Modules:
  0.0 350.8 jit_solution(13862374390926305704)
XLA Ops:
  6.5 0.8 iota_compare_fusion.1
  7.6 1.2 fusion.18
  8.9 1.3 convolution_convert_fusion
  10.2 7.7 %fusion.15 = bf16[1,4,16384]{2,1,0:T(4,128)(2,1)} fusion(bf16[128,1,512,128]{3,2,1,0:T(8,128)(2,1)} %param.16, bf16[4,128,512]{2,1,0:T(8,128)(2,1)S(1)} %convolution_convert_fusion), kind=kOutput, calls=%fused_computation.13 | convolution fusion | flops 67174400 | bytes 17432576 | tf_op jit(solution)/shard_map/bhc,hcv->bhv/dot_general | solution.py:111
  18.0 0.7 all-gather.12.cloned.1.call-update
  18.7 43.5 %all-gather.10.cloned.1.call-done = bf16[16,4,16384]{2,1,0:T(4,128)(2,1)} async-done(((bf16[1,4,16384]{2,1,0:T(4,128)(2,1)}), bf16[16,4,16384]{2,1,0:T(4,128)(2,1)}) %all-gather.10.cloned.1.call-update) | async-done | bytes 2097168 | tf_op jit(solution)/shard_map/all_gather | solution.py:115
  62.2 2.5 reshape.63.x_ref
  64.8 5.2 %copy-done.2 = bf16[128,1,128,448]{2,3,1,0:T(8,128)(2,1)S(1)} copy-done((bf16[128,1,128,448]{2,3,1,0:T(8,128)(2,1)S(1)}, bf16[128,1,128,448]{2,3,1,0:T(8,128)(2,1)}, u32[]{:S(2)}) %copy-start.2) | copy-done | bytes 14680088
  69.9 7.0 %project.1 = f32[64,448]{1,0:T(8,128)S(1)} custom-call(bf16[64,16384]{1,0:T(8,128)(2,1)S(1)} %reshape.63.x_ref, bf16[128,448,128]{2,1,0:T(8,128)(2,1)S(1)} %bitcast.45), custom_call_target="tpu_custom_call" | custom-call | flops 939524096 | bytes 16777216 | tf_op jit(solution)/shard_map/project/pallas_call | solution.py:47
  77.0 0.6 convert_element_type.50
  78.5 39.9 %all-gather.3 = f32[32,4,32]{2,1,0:T(4,128)S(1)} all-gather(f32[1,4,32]{2,1,0:T(4,128)S(1)} %convert_bitcast_fusion), channel_id=1, replica_groups=mesh['sec'=2,'grp'=16,'tp'=1] {'sec','grp','tp'}, dimensions={0}, use_global_device_ids=true | all-gather | bytes 16896 | tf_op jit(solution)/shard_map/all_gather | solution.py:91
  118.7 20.1 %copy.23 = bf16[896,8,2,1024]{3,1,2,0:T(8,128)(2,1)} copy(bf16[896,8,2,1024]{3,2,1,0:T(2,128)(2,1)} %bitcast.47) | data formatting | bytes 58720256
  138.8 4.3 %reshape.69 = f32[128,7168]{1,0:T(8,128)} reshape(bf16[32,4,7168]{2,1,0:T(4,128)(2,1)} %all-gather.12.cloned.1.call-done) | data formatting | bytes 5505024 | tf_op jit(solution)/shard_map/convert_element_type | solution.py:127
  143.1 34.9 %all-gather.8.cloned.1.call-done = bf16[2048,448]{1,0:T(8,128)(2,1)} async-done(((bf16[64,448]{1,0:T(8,128)(2,1)}), bf16[2048,448]{1,0:T(8,128)(2,1)}) %all-gather.8.cloned.1.call-update) | async-done | bytes 1835024 | tf_op jit(solution)/shard_map/all_gather | solution.py:120
  178.0 4.0 %copy.21 = bf16[2,64,16,448]{3,2,1,0:T(8,128)(2,1)} copy(bf16[2,64,16,448]{3,1,2,0:T(8,128)(2,1)} %bitcast.48) | data formatting | bytes 3670016 | tf_op jit(solution)/shard_map/transpose | solution.py:124
  182.0 3.8 %reshape.59 = bf16[128,7168]{1,0:T(8,128)(2,1)S(1)} reshape(bf16[2,64,16,448]{3,2,1,0:T(8,128)(2,1)} %copy.21) | data formatting | bytes 3670016 | tf_op jit(solution)/shard_map/reshape | solution.py:125
  185.8 2.7 multiply_reduce_fusion
  188.6 0.4 copy-done.3
  188.9 0.6 multiply_convert_fusion
  189.5 11.6 %fusion.36 = f32[128,2048]{1,0:T(8,128)S(1)} fusion(bf16[128,7168]{1,0:T(8,128)(2,1)S(1)} %multiply_convert_fusion, bf16[7168,2048]{1,0:T(8,128)(2,1)} %bitcast.46), kind=kOutput, calls=%fused_computation.44 | convolution fusion | flops 3758096384 | bytes 32243712 | tf_op jit(solution)/shard_map/dot_general | solution.py:145
  201.1 0.8 fusion.35
  202.0 8.6 %fusion.8 = bf16[128,7168]{1,0:T(8,128)(2,1)} fusion(bf16[1,1024,7168]{2,1,0:T(8,128)(2,1)} %param.23, f32[128]{0:T(128)S(1)} %select_reduce_fusion, f32[128,2048]{1,0:T(8,128)S(1)} %fusion.36), kind=kOutput, calls=%fused_computation.6 | convolution fusion | flops 1881669632 | bytes 17564160 | tf_op jit(solution)/shard_map/dot_general | solution.py:151
  210.7 132.0 %all-reduce.3.cloned.1.call-done = bf16[128,7168]{1,0:T(8,128)(2,1)} async-done(((bf16[128,7168]{1,0:T(8,128)(2,1)}), bf16[128,7168]{1,0:T(8,128)(2,1)}) %all-reduce.3.cloned.1.call-update) | async-done | bytes 1835024
  342.6 1.6 add_convert_fusion
  (33 shorter events, 1.1 us)
Async XLA Ops:
  6.5 1.1 copy-start
  6.5 55.7 %all-gather.10.cloned.1.call-start = ((), (), s32[]{:S(2)}) async-start(), calls=%async_computation.1 | async-start | bytes 2228224 | tf_op jit(solution)/shard_map/all_gather | solution.py:115
  17.9 120.9 %all-gather.12.cloned.1.call-start = ((), (), s32[]{:S(2)}) async-start(), calls=%async_computation.2 | async-start | bytes 1892352 | tf_op jit(solution)/shard_map/all_gather | solution.py:92
  18.7 159.3 %all-gather.8.cloned.1.call-start = ((), (), s32[]{:S(2)}) async-start(), calls=%async_computation | async-start | bytes 2162688 | tf_op jit(solution)/shard_map/all_gather | solution.py:120
  64.7 5.2 %copy-start.2 = (bf16[128,1,128,448]{2,3,1,0:T(8,128)(2,1)S(1)}, bf16[128,1,128,448]{2,3,1,0:T(8,128)(2,1)}, u32[]{:S(2)}) copy-start(bf16[128,1,128,448]{2,3,1,0:T(8,128)(2,1)} %param.17) | copy-start | bytes 44040196
  69.9 8.4 %copy-start.7 = (s32[4,8]{1,0:T(4,128)S(1)}, s32[4,8]{1,0:T(4,128)}, u32[]{:S(2)}) copy-start(s32[4,8]{1,0:T(4,128)} %param.20) | copy-start | bytes 388
  77.6 265.0 %all-reduce.3.cloned.1.call-start = ((), (), s32[]{:S(2)}) async-start(), calls=%async_computation.3 | async-start | bytes 3670016
  185.8 3.1 copy-start.3
  185.8 3.1 copy-start.6
  189.5 11.6 %copy-start.4 = (bf16[7168,32]{0,1:T(8,128)(2,1)S(1)}, bf16[7168,32]{0,1:T(8,128)(2,1)}, u32[]{:S(2)}) copy-start(bf16[7168,32]{0,1:T(8,128)(2,1)} %param.19) | copy-start | bytes 1376260
  202.0 140.6 %copy-start.5 = (bf16[4,7168]{1,0:T(4,128)(2,1)S(1)}, bf16[4,7168]{1,0:T(4,128)(2,1)}, u32[]{:S(2)}) copy-start(bf16[4,7168]{1,0:T(4,128)(2,1)} %param.12) | copy-start | bytes 172036
  202.0 142.2 %copy-start.1 = (bf16[4,128,1,576]{1,3,2,0:T(8,128)(2,1)S(1)}, bf16[4,128,1,576]{1,3,2,0:T(8,128)(2,1)}, u32[]{:S(2)}) copy-start(bf16[4,128,1,576]{1,3,2,0:T(8,128)(2,1)} %param.13) | copy-start | bytes 1769476
Sparse Core Ops, SparseCore 0:
  18.1 44.0 all-gather.9
  65.1 54.5 all-gather.11
  122.5 55.3 all-gather.7
  210.8 131.8 all-reduce.2

commit v2 on v0

--- a/solution.py
+++ b/solution.py
@@ -1,10 +1,421 @@
+import functools
+
 import jax
 import jax.numpy as jnp
 from jax import lax
+from jax.experimental import pallas as pl
+from jax.experimental.pallas import tpu as pltpu
 from jax.sharding import PartitionSpec as P
 
 score_scale = 192.0 ** (-0.5)
 route_scale = 2.5
+
+
+def divisor_at_most(number, most):
+    return max(d for d in range(1, most + 1) if number % d == 0)
+
+
+def project_kernel(heads_step, x_ref, w_ref, out_ref, total):
+    step = pl.program_id(0)
+
+    @pl.when(step == 0)
+    def _():
+        total[...] = jnp.zeros_like(total)
+
+    value_width = w_ref.shape[2]
+    part = jnp.zeros(total.shape, jnp.float32)
+    pair = 2 if heads_step % 2 == 0 else 1
+    for i in range(0, heads_step, pair):
+        block = jnp.concatenate([w_ref[i + k] for k in range(pair)], axis=1)
+        part += lax.dot_general(
+            x_ref[:, i * value_width : (i + pair) * value_width],
+            block,
+            (((1,), (1,)), ((), ())),
+            preferred_element_type=jnp.float32,
+        )
+    total[...] += part
+
+    @pl.when(step == pl.num_programs(0) - 1)
+    def _():
+        out_ref[...] = total[...].astype(out_ref.dtype)
+
+
+def project(rows, weight):
+    heads, columns, value_width = weight.shape
+    tokens = rows.shape[0]
+    heads_step = divisor_at_most(heads, 8)
+    return pl.pallas_call(
+        functools.partial(project_kernel, heads_step),
+        grid=(heads // heads_step,),
+        in_specs=[
+            pl.BlockSpec((tokens, heads_step * value_width), lambda i: (0, i)),
+            pl.BlockSpec((heads_step, columns, value_width), lambda i: (i, 0, 0)),
+        ],
+        out_specs=pl.BlockSpec((tokens, columns), lambda i: (0, 0)),
+        out_shape=jax.ShapeDtypeStruct((tokens, columns), jnp.float32),
+        scratch_shapes=[pltpu.VMEM((tokens, columns), jnp.float32)],
+        compiler_params=pltpu.CompilerParams(vmem_limit_bytes=16 * 1024 * 1024),
+        cost_estimate=pl.CostEstimate(
+            flops=2 * tokens * heads * value_width * columns,
+            bytes_accessed=2 * heads * value_width * (columns + tokens),
+            transcendentals=0,
+        ),
+        name="project",
+    )(rows, weight)
+
+MESH = pl.DeviceIdType.MESH
+
+
+def flip(index, bit):
+    return index + bit - 2 * bit * lax.rem(index // bit, 2)
+
+
+def partner(bit):
+    axis, value = bit
+    return {axis: flip(lax.axis_index(axis), value)}
+
+
+def greet(bits):
+    barrier = pltpu.get_barrier_semaphore()
+    for bit in bits:
+        pl.semaphore_signal(barrier, inc=1, device_id=partner(bit), device_id_type=MESH)
+    pl.semaphore_wait(barrier, len(bits))
+
+
+def axis_bits(axis, size):
+    return [(axis, 1 << k) for k in reversed(range(size.bit_length() - 1))]
+
+
+def gather_kernel(orders, spans, flat, x_ref, out_ref, send_sems, recv_sems, own_sem):
+    bits = orders[0]
+    greet(bits)
+
+    def block(subset, order):
+        place = {axis: lax.axis_index(axis) for axis in flat}
+        for k, (axis, value) in enumerate(order):
+            if subset >> k & 1:
+                place[axis] = flip(place[axis], value)
+        index = 0
+        for axis, size in flat.items():
+            index = index * size + place[axis]
+        return index
+
+    def move(chunk, order, step, subset):
+        first, count = spans[chunk]
+        slot = out_ref.at[block(subset, order), pl.ds(first, count)]
+        source = x_ref.at[pl.ds(first, count)] if subset == 0 else slot
+        which = (1 << step) - 1 + subset
+        return pltpu.make_async_remote_copy(
+            src_ref=source,
+            dst_ref=slot,
+            send_sem=send_sems.at[chunk, which],
+            recv_sem=recv_sems.at[chunk, which],
+            device_id=partner(order[step]),
+            device_id_type=MESH,
+        )
+
+    for step in range(len(bits)):
+        for chunk, order in enumerate(orders):
+            move(chunk, order, step, 0).start()
+    own = pltpu.make_async_copy(x_ref, out_ref.at[block(0, bits)], own_sem)
+    own.start()
+    for step in range(len(bits)):
+        for subset in range(1 << step):
+            for chunk, order in enumerate(orders):
+                move(chunk, order, step, subset).wait_recv()
+                for later in range(step + 1, len(bits)):
+                    move(chunk, order, later, subset + (1 << step)).start()
+    for step in range(len(bits)):
+        for subset in range(1 << step):
+            for chunk, order in enumerate(orders):
+                move(chunk, order, step, subset).wait_send()
+    own.wait()
+
+
+def gather(block, orders, flat, collective_id, name):
+    rows, columns = block.shape
+    blocks = 1
+    for size in flat.values():
+        blocks *= size
+    count = rows // len(orders)
+    spans = [(k * count, count) for k in range(len(orders))]
+    return pl.pallas_call(
+        functools.partial(gather_kernel, orders, spans, flat),
+        out_shape=jax.ShapeDtypeStruct((blocks, rows, columns), block.dtype),
+        in_specs=[pl.BlockSpec(memory_space=pltpu.VMEM)],
+        out_specs=pl.BlockSpec(memory_space=pltpu.VMEM),
+        scratch_shapes=[
+            pltpu.SemaphoreType.DMA((len(orders), blocks - 1)),
+            pltpu.SemaphoreType.DMA((len(orders), blocks - 1)),
+            pltpu.SemaphoreType.DMA,
+        ],
+        compiler_params=pltpu.CompilerParams(
+            collective_id=collective_id, has_side_effects=True, vmem_limit_bytes=40 * 1024 * 1024
+        ),
+        name=name,
+    )(block)
+
+
+def reduce_kernel(core, halving, whole_bits, orders, x_ref, out_ref, summed, from_core, half_in,
+                  whole_in, core_sems, half_sems, whole_sems, end_sems):
+    greet([core] + halving + whole_bits)
+    groups, rows, width = x_ref.shape
+    half = width // 2
+    part = half // len(orders)
+    side = lax.rem(lax.axis_index(core[0]) // core[1], 2)
+    mine = pl.ds(pl.multiple_of(side * half, 128), half)
+    other = pl.ds(pl.multiple_of((1 - side) * half, 128), half)
+    my_bit = {bit: lax.rem(lax.axis_index(bit[0]) // bit[1], 2) for bit in halving}
+
+    def group_of(done, current, sent, rest):
+        index, place = 0, 0
+        for bit in halving:
+            if bit in done:
+                value = my_bit[bit]
+            elif bit == current:
+                value = (1 - my_bit[bit]) if sent else my_bit[bit]
+            else:
+                value = rest >> place & 1
+                place += 1
+            index = index * 2 + value
+        return index
+
+    def remote(source, target, sems, device):
+        return pltpu.make_async_remote_copy(
+            src_ref=source, dst_ref=target, send_sem=sems.at[0], recv_sem=sems.at[1],
+            device_id=partner(device), device_id_type=MESH,
+        )
+
+    def add(first, second):
+        return (first.astype(jnp.float32) + second.astype(jnp.float32)).astype(jnp.bfloat16)
+
+    pending = []
+    firsts = [
+        remote(x_ref.at[g, :, other], from_core.at[g], core_sems.at[g], core)
+        for g in range(groups)
+    ]
+    for copy in firsts:
+        copy.start()
+    for g in range(groups):
+        firsts[g].wait_recv()
+        summed[g] = add(x_ref[g, :, mine], from_core[g])
+    pending += firsts
+    steps = len(halving)
+    slots = [0]
+    for step in range(steps):
+        slots.append(slots[-1] + (1 << (steps - 1 - step)))
+
+    def halve(step, chunk, rest):
+        order = orders[chunk]
+        span = pl.ds(chunk * part, part)
+        slot = slots[step] + rest
+        return remote(
+            summed.at[group_of(order[:step], order[step], True, rest), :, span],
+            half_in.at[slot, :, span],
+            half_sems.at[chunk, slot],
+            order[step],
+        )
+
+    for step in range(steps):
+        for chunk in range(len(orders)):
+            for rest in range(1 << (steps - 1 - step)):
+                copy = halve(step, chunk, rest)
+                copy.start()
+                pending.append(copy)
+        for chunk, order in enumerate(orders):
+            span = pl.ds(chunk * part, part)
+            for rest in range(1 << (steps - 1 - step)):
+                halve(step, chunk, rest).wait_recv()
+                g = group_of(order[:step], order[step], False, rest)
+                summed[g, :, span] = add(
+                    summed[g, :, span], half_in[slots[step] + rest, :, span]
+                )
+    group = group_of(halving, None, False, 0)
+    current = summed[group]
+    for k, bit in enumerate(whole_bits):
+        whole_in[k, 0] = current
+        copy = remote(whole_in.at[k, 0], whole_in.at[k, 1], whole_sems.at[k], bit)
+        copy.start()
+        copy.wait_recv()
+        pending.append(copy)
+        current = add(whole_in[k, 0], whole_in[k, 1])
+    out_ref[:, mine] = current
+    last = remote(out_ref.at[:, mine], out_ref.at[:, mine], end_sems, core)
+    last.start()
+    last.wait_recv()
+    pending.append(last)
+    for copy in pending:
+        copy.wait_send()
+
+
+def reduce_rows(values, core, halving, whole_bits, orders, collective_id):
+    groups, rows, width = values.shape
+    half = width // 2
+    dma = pltpu.SemaphoreType.DMA
+    return pl.pallas_call(
+        functools.partial(reduce_kernel, core, halving, whole_bits, orders),
+        out_shape=jax.ShapeDtypeStruct((rows, width), values.dtype),
+        in_specs=[pl.BlockSpec(memory_space=pltpu.VMEM)],
+        out_specs=pl.BlockSpec(memory_space=pltpu.VMEM),
+        scratch_shapes=[
+            pltpu.VMEM((groups, rows, half), jnp.bfloat16),
+            pltpu.VMEM((groups, rows, half), jnp.bfloat16),
+            pltpu.VMEM((groups - 1, rows, half), jnp.bfloat16),
+            pltpu.VMEM((len(whole_bits), 2, rows, half), jnp.bfloat16),
+            dma((groups, 2)),
+            dma((len(orders), groups - 1, 2)),
+            dma((len(whole_bits), 2)),
+            dma((2,)),
+        ],
+        compiler_params=pltpu.CompilerParams(
+            collective_id=collective_id, has_side_effects=True, vmem_limit_bytes=56 * 1024 * 1024
+        ),
+        name="reduce_rows",
+    )(values)
+
+
+def shards(
+    hidden_in,
+    queries,
+    latent_cache,
+    lengths,
+    w_uv,
+    attn_weight,
+    norm_gain,
+    router,
+    routes,
+    live_counts,
+    expert_in,
+    expert_out,
+):
+    own_tokens, width = hidden_in.shape
+    sections = lax.axis_size("sec")
+    expert_groups = lax.axis_size("grp")
+    latent_width = w_uv.shape[2]
+    experts = router.shape[1]
+
+    tp = lax.axis_size("tp")
+    grp_bits = axis_bits("grp", expert_groups)
+    sec_bits = axis_bits("sec", sections)
+    core, low, rest_bits = grp_bits[-1], grp_bits[-2], grp_bits[:-2]
+    flat = {"sec": sections, "grp": expert_groups}
+
+    picked = jnp.any(routes[:, :, None] == jnp.arange(experts)[None, None, :], axis=1)
+    living = jnp.arange(own_tokens) < live_counts[0]
+    unit_mask = (picked & living[:, None]).astype(jnp.bfloat16)
+    unit_hidden = hidden_in
+    if tp > 1:
+        unit_mask = lax.all_gather(unit_mask, "tp", axis=0, tiled=True)
+        unit_hidden = lax.all_gather(unit_hidden, "tp", axis=0, tiled=True)
+    unit = unit_hidden.shape[0]
+    hidden_part = lax.all_to_all(unit_hidden, "grp", split_axis=1, concat_axis=0, tiled=True)
+
+    query_block = queries[:, :, 0, :]
+    scores = (
+        jnp.einsum("bhr,bpr->bhp", query_block, latent_cache, preferred_element_type=jnp.float32)
+        * score_scale
+    )
+    positions = jnp.arange(latent_cache.shape[1])
+    visible = positions[None, None, :] < lengths[:, None, None]
+    scores = jnp.where(visible, scores, -1e30)
+    highest = jnp.max(scores, axis=2, keepdims=True)
+    raised = jnp.exp(scores - highest)
+    softmax_weights = (raised / jnp.sum(raised, axis=2, keepdims=True)).astype(jnp.bfloat16)
+    latent_out = jnp.einsum(
+        "bhp,bpc->bhc",
+        softmax_weights,
+        latent_cache[:, :, :latent_width],
+        preferred_element_type=jnp.float32,
+    ).astype(jnp.bfloat16)
+    head_out = jnp.einsum(
+        "bhc,hcv->bhv", latent_out, w_uv[:, 0], preferred_element_type=jnp.float32
+    ).astype(jnp.bfloat16)
+    parts = max(1, 32 // unit)
+    head_rows = head_out.reshape(unit, parts, -1).transpose(1, 0, 2).reshape(parts * unit, -1)
+    group_blocks = gather(
+        head_rows,
+        [rest_bits + [low, core], rest_bits + [low, core]],
+        {"grp": expert_groups},
+        0,
+        "gather_heads",
+    )
+    group_rows = (
+        group_blocks.reshape(expert_groups, parts, unit, -1)
+        .transpose(0, 2, 1, 3)
+        .reshape(expert_groups * unit, -1)
+    )
+    column_part = project(group_rows, jnp.transpose(attn_weight[:, 0], (0, 2, 1)))
+    if lax.axis_size("tp") > 1:
+        column_part = lax.psum(column_part, "tp")
+    column_part = column_part.astype(jnp.bfloat16).astype(jnp.float32)
+    residual_part = (column_part + hidden_part.astype(jnp.float32)).astype(jnp.bfloat16)
+    section_tokens, columns = residual_part.shape
+    mask_block = jnp.pad(unit_mask, ((0, section_tokens - unit), (0, 0)))
+    gathered = gather(
+        jnp.concatenate([residual_part, mask_block], axis=1),
+        [rest_bits + [low] + sec_bits + [core], sec_bits + [low] + rest_bits + [core]],
+        flat,
+        1,
+        "gather_columns",
+    )
+    depth = len(grp_bits) - 1
+
+    def reorder(rows):
+        split = rows.reshape([sections] + [2] * depth + [2 * unit, rows.shape[-1]])
+        turned = split.transpose([0] + list(range(depth, 0, -1)) + [depth + 1, depth + 2])
+        return turned.reshape(-1, rows.shape[-1])
+
+    mask_all = reorder(gathered[:, :unit, columns:].reshape(-1, experts)).astype(jnp.float32)
+    residual = (
+        gathered[:, :, :columns]
+        .reshape([sections, expert_groups] + [2] * depth + [2 * unit, columns])
+        .transpose([0] + list(range(depth + 1, 1, -1)) + [depth + 2, 1, depth + 3])
+        .reshape(sections * section_tokens, width)
+        .astype(jnp.float32)
+    )
+    normed = (
+        residual
+        * lax.rsqrt(jnp.mean(residual * residual, axis=1, keepdims=True) + 1e-06)
+        * norm_gain
+    ).astype(jnp.bfloat16)
+    affinity = jax.nn.sigmoid(jnp.dot(normed, router, preferred_element_type=jnp.float32))
+    chosen = affinity * mask_all
+    live_all = jnp.max(mask_all, axis=1, keepdims=True) > 0.0
+    gate_all = jnp.where(
+        live_all, route_scale * chosen / jnp.sum(chosen, axis=1, keepdims=True), 0.0
+    )
+    group = lax.axis_index("sec") * expert_groups + lax.axis_index("grp")
+    own_gate = jnp.sum(
+        jnp.where(jnp.arange(experts)[None, :] == group, gate_all, 0.0), axis=1, keepdims=True
+    )
+
+    slice_width = expert_in.shape[3]
+    gate_up = jnp.dot(
+        normed, expert_in[0].reshape(width, 2 * slice_width), preferred_element_type=jnp.float32
+    )
+    activated = (jax.nn.silu(gate_up[:, :slice_width]) * gate_up[:, slice_width:]).astype(
+        jnp.bfloat16
+    )
+    value = jnp.dot(activated, expert_out[0], preferred_element_type=jnp.float32)
+    mixed = (value * own_gate).astype(jnp.bfloat16)
+    grain = 4 * unit
+    halving = sec_bits + [low] + list(reversed(rest_bits))[:-1]
+    swapped = [low] + sec_bits + list(reversed(rest_bits))[:-1]
+    mixed = mixed.reshape(-1, grain, width)
+    shared = reduce_rows(mixed, core, halving, rest_bits[:1], [halving, swapped], 2)
+    place = lax.axis_index("grp")
+    quarter = (place // rest_bits[0][1]) % 2 * 2 + place % 2
+    if tp > 1:
+        owned = lax.dynamic_slice_in_dim(shared, quarter * unit, unit, 0)
+        expert_mix = lax.psum_scatter(owned, "tp", scatter_dimension=0, tiled=True)
+    else:
+        expert_mix = lax.dynamic_slice_in_dim(shared, quarter * unit, unit, 0)
+    own_row = 0
+    for axis, value in halving + rest_bits[:1]:
+        own_row = own_row * 2 + (lax.axis_index(axis) // value) % 2
+    own_row = (own_row * 2 + place % 2) * unit + lax.axis_index("tp") * own_tokens
+    own_residual = lax.dynamic_slice_in_dim(residual, own_row, own_tokens, 0)
+    return (own_residual + expert_mix.astype(jnp.float32)).astype(jnp.bfloat16)
 
 
 def expert_slice(rows_in, expert_in, expert_out):
@@ -21,7 +432,7 @@
     )
 
 
-def shards(
+def shards_split(
     hidden_in,
     queries,
     latent_cache,
@@ -155,6 +566,7 @@
         P(("sec", "grp"), None, None, "tp"),
         P(("sec", "grp"), "tp", None),
     )
+    body = shards_split if mesh.shape["tp"] > 1 else shards
     return jax.shard_map(
-        shards, mesh=mesh, in_specs=placed, out_specs=P(("sec", "grp", "tp"), None), check_vma=False
-    )
+        body, mesh=mesh, in_specs=placed, out_specs=P(("sec", "grp", "tp"), None), check_vma=False
+    )

time: 208 us -> 179 us (0.86)
  Pallas kernels: 0 us -> 74.4 us
  blocking collectives: 59 us -> 0 us
  local copies, waits for them, and re-layouts: 73.8 us -> 47.2 us
  other arithmetic: 1.76 us -> 17.3 us
  between operations: 14.3 us -> 0.96 us
  waiting for transfers between devices: 11.6 us -> 0.01 us
  matrix products: 38.2 us -> 30.8 us
    pallas_call x0 -> x4, Pallas kernels: none -> 74.4 us  [the longest x2 39.7 us: gather(): pl.pallas_call(functools.partial(gather_kernel, orders, spans, flat), out...]
    all_to_all x3 -> x0, blocking collectives: 59 us -> none  [the longest x1 28.5 us: shards(): lax.all_to_all(own_sums.astype(jnp.bfloat16), 'grp', split_axis=1, concat...]
    another operation x1, local copies, waits for them, and re-layouts: 22.4 us -> 0.01 us  [reorder(): split = rows.reshape([sections] + [2] * depth + [2 * unit, rows.shape[-1]])]
    unnamed x22 -> x14, local copies, waits for them, and re-layouts: 37.8 us -> 26.4 us
    convert_element_type x3 -> x6, other arithmetic: 0.19 us -> 10.6 us  [the longest x1 6.36 us: shards(): normed = (residual * lax.rsqrt(jnp.mean(residual * residual, axis=1, keep...]
    convert_element_type x5, local copies, waits for them, and re-layouts: 3.82 us -> 12.7 us  [the longest x2 8.81 us: shards(): residual = gathered[:, :, :columns].reshape([sections, expert_groups] + [...]
    all_to_all x2 -> x1, waiting for transfers between devices: 7.29 us -> 0.01 us  [shards(): lax.all_to_all(unit_hidden, 'grp', split_axis=1, concat_axis=0, tiled=True)]
    dot_general x6 -> x3, matrix products: 28 us -> 21.3 us  [the longest x1 11.8 us: shards(): jnp.dot(normed, expert_in[0].reshape(width, 2 * slice_width), preferred_e...]
  transfers between devices with their start and end apart: 3 -> 1, of which waited for: 3 -> 0; matrix products, arithmetic and copies ran while one was open for 29% -> 22% of each run, Pallas kernels for 0% -> 16%
where the time goes in v2:
time: 179 us; the launch traced here: 178 us
  Pallas kernels  74.4 us (42%)
  local copies, waits for them, and re-layouts  47.2 us (26%)
  matrix products  30.8 us (17%)
  other arithmetic  17.3 us (10%)
  starting transfers between devices  7.39 us (4%)
    pallas_call x2, Pallas kernels, gather(): pl.pallas_call(functools.partial(gather_kernel, orders, spans, flat), out...  39.7 us
    pallas_call x1, Pallas kernels, reduce_rows(): pl.pallas_call(functools.partial(reduce_kernel, core, halving, whole_bits...  27.6 us
    unnamed x14, local copies, waits for them, and re-layouts  26.4 us
    dot_general x1, matrix products, shards(): jnp.dot(normed, expert_in[0].reshape(width, 2 * slice_width), preferred_e...  11.8 us
    convert_element_type x2, local copies, waits for them, and re-layouts, shards(): residual = gathered[:, :, :columns].reshape([sections, expert_groups] + [...  8.81 us
    dot_general x1, matrix products, shards(): jnp.dot(activated, expert_out[0], preferred_element_type=jnp.float32)  8.61 us
    all_to_all x1, starting transfers between devices, shards(): lax.all_to_all(unit_hidden, 'grp', split_axis=1, concat_axis=0, tiled=True)  7.39 us
    dot_general x1, matrix products, shards(): jnp.einsum('bhc,hcv->bhv', latent_out, w_uv[:, 0], preferred_element_type...  7.07 us
  transfers between devices with their start and end apart: 1, of which 0 were waited for; matrix products, arithmetic and copies ran while one was open for 22% of the time, Pallas kernels for 16%

profile of v2, /device:TPU:0, one launch (start us, length us, event | category | flops | bytes accessed | tf_op | source)
XLA Modules:
  0.0 178.0 jit_solution(15614580363167588297)
XLA Ops:
  0.0 1.0 all_to_all.10
  1.7 7.4 %all-to-all-start = ((bf16[4,16,448]{2,0,1:T(4,128)(2,1)}), bf16[4,16,448]{2,0,1:T(4,128)(2,1)S(1)}, u32[]{:S(2)}, u32[]{:S(2)}) async-start(bf16[4,16,448]{2,0,1:T(4,128)(2,1)} %copy.24), calls=%async_computation | async-start | bytes 131072 | tf_op jit(solution)/shard_map/all_to_all | solution.py:311
  12.3 1.2 fusion.18
  13.5 1.3 convolution_convert_fusion
  14.8 7.1 %fusion.15 = bf16[128,4,128]{2,1,0:T(4,128)(2,1)S(1)} fusion(bf16[128,1,512,128]{3,2,1,0:T(8,128)(2,1)} %param.16, bf16[4,128,512]{2,1,0:T(8,128)(2,1)S(1)} %convolution_convert_fusion), kind=kOutput, calls=%fused_computation.16 | convolution fusion | flops 67174400 | bytes 17432576 | tf_op jit(solution)/shard_map/bhc,hcv->bhv/dot_general | solution.py:330
  22.0 21.7 %gather_heads.1 = bf16[16,32,2048]{2,1,0:T(8,128)(2,1)S(1)} custom-call(bf16[32,2048]{1,0:T(8,128)(2,1)S(1)} %reshape.108.x_ref), custom_call_target="tpu_custom_call" | custom-call | tf_op jit(solution)/shard_map/gather_heads/pallas_call | solution.py:142
  43.6 2.2 %reshape.109 = bf16[16,8,4,2048]{3,2,1,0:T(4,128)(2,1)} reshape(bf16[16,32,2048]{2,1,0:T(8,128)(2,1)S(1)} %gather_heads.1) | data formatting | bytes 4194304 | tf_op jit(solution)/shard_map/reshape | solution.py:343
  45.9 3.0 %copy.23 = bf16[16,8,4,2048]{3,1,2,0:T(8,128)(2,1)S(1)} copy(bf16[16,8,4,2048]{3,2,1,0:T(4,128)(2,1)} %reshape.109) | data formatting | bytes 4194304 | tf_op jit(solution)/shard_map/reshape | solution.py:343
  48.9 1.2 copy.28
  50.1 20.0 %copy.29 = bf16[896,8,2,1024]{3,1,2,0:T(8,128)(2,1)} copy(bf16[896,8,2,1024]{3,2,1,0:T(2,128)(2,1)} %bitcast.67) | data formatting | bytes 58720256
  70.1 5.2 %copy-done.2 = bf16[128,1,128,448]{2,3,1,0:T(8,128)(2,1)S(1)} copy-done((bf16[128,1,128,448]{2,3,1,0:T(8,128)(2,1)S(1)}, bf16[128,1,128,448]{2,3,1,0:T(8,128)(2,1)}, u32[]{:S(2)}) %copy-start.2) | copy-done | bytes 14680088
  75.3 7.0 %project.1 = f32[64,448]{1,0:T(8,128)S(1)} custom-call(bf16[64,16384]{1,0:T(8,128)(2,1)S(1)} %bitcast.65, bf16[128,448,128]{2,1,0:T(8,128)(2,1)S(1)} %bitcast.64), custom_call_target="tpu_custom_call" | custom-call | flops 939524096 | bytes 16777216 | tf_op jit(solution)/shard_map/project/pallas_call | solution.py:47
  82.5 18.1 %gather_columns.1 = bf16[32,64,480]{2,1,0:T(8,128)(2,1)S(1)} custom-call(bf16[64,480]{1,0:T(8,128)(2,1)S(1)} %pad_maximum_fusion.x_ref), custom_call_target="tpu_custom_call" | custom-call | tf_op jit(solution)/shard_map/gather_columns/pallas_call | solution.py:142
  100.8 2.6 %convert.17 = f32[2,16,2,2,2,8,448]{6,5,4,3,2,1,0:T(8,128)} convert(bf16[2,16,2,2,2,8,448]{6,5,4,3,2,1,0:T(8,128)(2,1)S(1)} %bitcast.62) | non-fusion elementwise | flops 917504 | bytes 5505024 | tf_op jit(solution)/shard_map/convert_element_type | solution.py:374
  103.5 3.2 %copy.38 = f32[2,16,2,2,2,8,448]{6,1,5,2,3,4,0:T(8,128)} copy(bf16[2,16,2,2,2,8,448]{6,5,4,3,2,1,0:T(8,128)(2,1)S(1)} %bitcast.63) | data formatting | bytes 5505024 | tf_op jit(solution)/shard_map/convert_element_type | solution.py:374
  106.8 4.7 %multiply_reduce_fusion = f32[2,2,2,2,8]{4,3,2,1,0:T(2,128)S(1)} fusion(f32[2,16,2,2,2,8,448]{6,5,4,3,2,1,0:T(8,128)} %convert.17), kind=kLoop, calls=%fused_computation.9 | loop fusion | flops 1834880 | bytes 3670528 | tf_op jit(solution)/shard_map/reduce_sum | solution.py:378
  111.6 6.4 %multiply_convert_fusion = bf16[2,2,2,2,8,16,448]{6,5,4,3,2,1,0:T(8,128)(2,1)} fusion(f32[16,448]{1,0:T(8,128)S(1)} %mul.94, f32[2,2,2,2,8]{4,3,2,1,0:T(2,128)S(1)} %add_rsqrt_fusion, f32[2,16,2,2,2,8,448]{6,5,4,3,2,1,0:T(8,128)} %convert.17), kind=kLoop, calls=%fused_computation.8 | loop fusion | flops 2752512 | bytes 5534208 | tf_op jit(solution)/shard_map/convert_element_type | solution.py:380
  118.0 3.8 %convert_element_type.93 = bf16[128,7168]{1,0:T(8,128)(2,1)S(1)} reshape(bf16[2,2,2,2,8,16,448]{6,5,4,3,2,1,0:T(8,128)(2,1)} %multiply_convert_fusion) | data formatting | bytes 3670016 | tf_op jit(solution)/shard_map/convert_element_type | solution.py:380
  121.7 5.6 %reshape.113 = f32[128,7168]{1,0:T(8,128)} reshape(f32[2,2,2,2,8,16,448]{6,5,4,3,2,1,0:T(8,128)} %bitcast.68) | data formatting | bytes 7340032 | tf_op jit(solution)/shard_map/convert_element_type | solution.py:374
  127.4 11.8 %fusion.37 = f32[128,2048]{1,0:T(8,128)S(1)} fusion(bf16[128,7168]{1,0:T(8,128)(2,1)S(1)} %convert_element_type.93, bf16[7168,2048]{1,0:T(8,128)(2,1)} %bitcast.66), kind=kOutput, calls=%fused_computation.53 | convolution fusion | flops 3758096384 | bytes 32243712 | tf_op jit(solution)/shard_map/dot_general | solution.py:393
  139.2 0.8 fusion.36
  140.2 8.6 %fusion.8 = bf16[128,7168]{1,0:T(8,128)(2,1)} fusion(bf16[1,1024,7168]{2,1,0:T(8,128)(2,1)} %param.23, f32[128]{0:T(128)S(1)} %select_reduce_fusion, f32[128,2048]{1,0:T(8,128)S(1)} %fusion.37), kind=kOutput, calls=%fused_computation.6 | convolution fusion | flops 1881669632 | bytes 17564160 | tf_op jit(solution)/shard_map/dot_general | solution.py:399
  148.8 27.6 %reduce_rows.1 = bf16[16,7168]{1,0:T(8,128)(2,1)} custom-call(bf16[8,16,7168]{2,1,0:T(8,128)(2,1)} %bitcast.70), custom_call_target="tpu_custom_call" | custom-call | tf_op jit(solution)/shard_map/reduce_rows/pallas_call | solution.py:255
  176.4 1.6 add_convert_fusion.1
  (36 shorter events, 3.9 us)
Async XLA Ops:
  0.0 12.2 %copy-start = (bf16[4,128,1,576]{1,3,2,0:T(8,128)(2,1)S(1)}, bf16[4,128,1,576]{1,3,2,0:T(8,128)(2,1)}, u32[]{:S(2)}) copy-start(bf16[4,128,1,576]{1,3,2,0:T(8,128)(2,1)} %param.13) | copy-start | bytes 1769476
  1.7 80.7 %all-to-all-start = ((bf16[4,16,448]{2,0,1:T(4,128)(2,1)}), bf16[4,16,448]{2,0,1:T(4,128)(2,1)S(1)}, u32[]{:S(2)}, u32[]{:S(2)}) async-start(bf16[4,16,448]{2,0,1:T(4,128)(2,1)} %copy.24), calls=%async_computation | async-start | bytes 131072 | tf_op jit(solution)/shard_map/all_to_all | solution.py:311
  70.1 5.2 %copy-start.2 = (bf16[128,1,128,448]{2,3,1,0:T(8,128)(2,1)S(1)}, bf16[128,1,128,448]{2,3,1,0:T(8,128)(2,1)}, u32[]{:S(2)}) copy-start(bf16[128,1,128,448]{2,3,1,0:T(8,128)(2,1)} %param.17) | copy-start | bytes 44040196
  127.4 11.8 %copy-start.3 = (f32[128,7168]{1,0:T(8,128)S(1)}, f32[128,7168]{1,0:T(8,128)}, u32[]{:S(2)}) copy-start(f32[128,7168]{1,0:T(8,128)} %reshape.113) | copy-start | bytes 11010052
  127.4 11.8 %copy-start.4 = (bf16[7168,32]{0,1:T(8,128)(2,1)S(1)}, bf16[7168,32]{0,1:T(8,128)(2,1)}, u32[]{:S(2)}) copy-start(bf16[7168,32]{0,1:T(8,128)(2,1)} %param.19) | copy-start | bytes 1376260
  127.4 11.8 %copy-start.5 = (f32[7168]{0:T(1024)S(1)}, f32[7168]{0:T(1024)}, u32[]{:S(2)}) copy-start(f32[7168]{0:T(1024)} %param.18) | copy-start | bytes 86020
  140.2 37.8 %copy-start.1 = (bf16[4,128,1,576]{1,3,2,0:T(8,128)(2,1)S(1)}, bf16[4,128,1,576]{1,3,2,0:T(8,128)(2,1)}, u32[]{:S(2)}) copy-start(bf16[4,128,1,576]{1,3,2,0:T(8,128)(2,1)} %param.13) | copy-start | bytes 1769476

commit v3 on v2

--- a/solution.py
+++ b/solution.py
@@ -274,6 +274,126 @@
     )(values)
 
 
+def norm_kernel(columns, turn, x_ref, gain_ref, normed_ref, residual_ref, held):
+    blocks, rows, _ = x_ref.shape
+    width = gain_ref.shape[1]
+    per = width // columns
+    small = rows // len(turn)
+    for section in range(blocks // per):
+        span = pl.ds(section * rows, rows)
+        squares = jnp.zeros((rows, 1), jnp.float32)
+        for place in range(per):
+            block = x_ref[section * per + place][:, :columns].astype(jnp.float32)
+            block = jnp.concatenate([block[g * small : (g + 1) * small] for g in turn], axis=0)
+            held[span, place * columns : (place + 1) * columns] = block
+            squares += jnp.sum(block * block, axis=1, keepdims=True)
+        scale = lax.rsqrt(squares / width + 1e-06)
+        step = 512 if width % 512 == 0 else 128
+        for first in range(0, width, step):
+            part = held[span, first : first + step]
+            residual_ref[span, first : first + step] = part.astype(jnp.bfloat16)
+            normed_ref[span, first : first + step] = (
+                part * scale * gain_ref[:, first : first + step]
+            ).astype(jnp.bfloat16)
+
+
+def norm_rows(gathered, gain, columns, turn):
+    blocks, rows, _ = gathered.shape
+    width = gain.shape[0]
+    total = blocks * rows * columns // width
+    vmem = pl.BlockSpec(memory_space=pltpu.VMEM)
+    shape = jax.ShapeDtypeStruct((total, width), jnp.bfloat16)
+    return pl.pallas_call(
+        functools.partial(norm_kernel, columns, turn),
+        out_shape=(shape, shape),
+        in_specs=[vmem, vmem],
+        out_specs=(vmem, vmem),
+        scratch_shapes=[pltpu.VMEM((total, width), jnp.float32)],
+        compiler_params=pltpu.CompilerParams(vmem_limit_bytes=32 * 1024 * 1024),
+        name="norm_rows",
+    )(gathered, gain[None, :])
+
+
+def hidden_kernel(deep, x_ref, w_ref, out_ref, held, total, sems):
+    depth = w_ref.shape[0]
+    tiles = w_ref.shape[1]
+    tokens = x_ref.shape[0]
+    steps = depth // deep
+
+    def fetch(step, slot):
+        return [
+            pltpu.make_async_copy(
+                w_ref.at[pl.ds(step * deep, deep), tile], held.at[slot, tile], sems.at[slot, tile]
+            )
+            for tile in range(tiles)
+        ]
+
+    slots = held.shape[0]
+    flat_held = held.reshape(slots, tiles, 2 * deep, 128)
+    for ahead in range(slots - 1):
+        for copy in fetch(ahead, ahead):
+            copy.start()
+    total[...] = jnp.zeros_like(total)
+    row = lax.broadcasted_iota(jnp.int32, (128, 256), 0)
+    column = lax.broadcasted_iota(jnp.int32, (128, 256), 1)
+    even = (column == 2 * row).astype(jnp.bfloat16)
+    odd = (column == 2 * row + 1).astype(jnp.bfloat16)
+
+    def body(step, carry):
+        slot = lax.rem(step, slots)
+
+        @pl.when(step + slots - 1 < steps)
+        def _():
+            for copy in fetch(step + slots - 1, lax.rem(step + slots - 1, slots)):
+                copy.start()
+
+        for copy in fetch(step, slot):
+            copy.wait()
+        spread = []
+        for k in range(deep // 128):
+            first = pl.multiple_of(step * deep + k * 128, 128)
+            x = x_ref[:, pl.ds(first, 128)]
+            both = [
+                jnp.dot(x, place, preferred_element_type=jnp.float32).astype(jnp.bfloat16)
+                for place in (even, odd)
+            ]
+            spread.append(jnp.concatenate(both, axis=0))
+        left = jnp.concatenate(spread, axis=1)
+        for tile in range(0, tiles, 2):
+            right = jnp.concatenate(
+                [flat_held[slot, tile + j] for j in range(2)], axis=1
+            )
+            total[:, tile * 128 : tile * 128 + 256] += jnp.dot(
+                left, right, preferred_element_type=jnp.float32
+            )
+        return carry
+
+    lax.fori_loop(0, steps, body, 0)
+    gate = total[:tokens, :]
+    out_ref[...] = (gate / (1.0 + jnp.exp(-gate)) * total[tokens:, :]).astype(out_ref.dtype)
+
+
+def hidden_units(rows, weight):
+    depth, _, slice_width = weight.shape
+    tokens = rows.shape[0]
+    deep, slots = 256, 3
+    tiles = slice_width // 128
+    lanes = weight.reshape(depth, 2, tiles, 128).transpose(0, 2, 1, 3)
+    return pl.pallas_call(
+        functools.partial(hidden_kernel, deep),
+        out_shape=jax.ShapeDtypeStruct((tokens, slice_width), jnp.bfloat16),
+        in_specs=[pl.BlockSpec(memory_space=pltpu.VMEM), pl.BlockSpec(memory_space=pl.ANY)],
+        out_specs=pl.BlockSpec(memory_space=pltpu.VMEM),
+        scratch_shapes=[
+            pltpu.VMEM((slots, tiles, deep, 2, 128), jnp.bfloat16),
+            pltpu.VMEM((2 * tokens, slice_width), jnp.float32),
+            pltpu.SemaphoreType.DMA((slots, tiles)),
+        ],
+        compiler_params=pltpu.CompilerParams(vmem_limit_bytes=40 * 1024 * 1024),
+        name="hidden_units",
+    )(rows, lanes)
+
+
 def shards(
     hidden_in,
     queries,
@@ -334,7 +454,7 @@
     head_rows = head_out.reshape(unit, parts, -1).transpose(1, 0, 2).reshape(parts * unit, -1)
     group_blocks = gather(
         head_rows,
-        [rest_bits + [low, core], rest_bits + [low, core]],
+        [rest_bits + [low, core], [low] + rest_bits + [core]],
         {"grp": expert_groups},
         0,
         "gather_heads",
@@ -366,18 +486,10 @@
         return turned.reshape(-1, rows.shape[-1])
 
     mask_all = reorder(gathered[:, :unit, columns:].reshape(-1, experts)).astype(jnp.float32)
-    residual = (
-        gathered[:, :, :columns]
-        .reshape([sections, expert_groups] + [2] * depth + [2 * unit, columns])
-        .transpose([0] + list(range(depth + 1, 1, -1)) + [depth + 2, 1, depth + 3])
-        .reshape(sections * section_tokens, width)
-        .astype(jnp.float32)
-    )
-    normed = (
-        residual
-        * lax.rsqrt(jnp.mean(residual * residual, axis=1, keepdims=True) + 1e-06)
-        * norm_gain
-    ).astype(jnp.bfloat16)
+    turn = [
+        sum(((g >> k) & 1) << (depth - 1 - k) for k in range(depth)) for g in range(1 << depth)
+    ]
+    normed, residual = norm_rows(gathered, norm_gain, columns, turn)
     affinity = jax.nn.sigmoid(jnp.dot(normed, router, preferred_element_type=jnp.float32))
     chosen = affinity * mask_all
     live_all = jnp.max(mask_all, axis=1, keepdims=True) > 0.0
@@ -389,13 +501,7 @@
         jnp.where(jnp.arange(experts)[None, :] == group, gate_all, 0.0), axis=1, keepdims=True
     )
 
-    slice_width = expert_in.shape[3]
-    gate_up = jnp.dot(
-        normed, expert_in[0].reshape(width, 2 * slice_width), preferred_element_type=jnp.float32
-    )
-    activated = (jax.nn.silu(gate_up[:, :slice_width]) * gate_up[:, slice_width:]).astype(
-        jnp.bfloat16
-    )
+    activated = hidden_units(normed, expert_in[0])
     value = jnp.dot(activated, expert_out[0], preferred_element_type=jnp.float32)
     mixed = (value * own_gate).astype(jnp.bfloat16)
     grain = 4 * unit
@@ -414,7 +520,7 @@
     for axis, value in halving + rest_bits[:1]:
         own_row = own_row * 2 + (lax.axis_index(axis) // value) % 2
     own_row = (own_row * 2 + place % 2) * unit + lax.axis_index("tp") * own_tokens
-    own_residual = lax.dynamic_slice_in_dim(residual, own_row, own_tokens, 0)
+    own_residual = lax.dynamic_slice_in_dim(residual, own_row, own_tokens, 0).astype(jnp.float32)
     return (own_residual + expert_mix.astype(jnp.float32)).astype(jnp.bfloat16)
 
 

time: 179 us -> 138 us (0.77)
  local copies, waits for them, and re-layouts: 47.2 us -> 13.7 us
  Pallas kernels: 74.4 us -> 98.6 us
  matrix products: 30.8 us -> 13.7 us
  other arithmetic: 17.3 us -> 3.57 us
    pallas_call x0 -> x2, Pallas kernels: none -> 26 us  [the longest x1 24.7 us: hidden_units(): pl.pallas_call(functools.partial(hidden_kernel, deep), out_shape=jax.Shap...]
    unnamed x14 -> x19, local copies, waits for them, and re-layouts: 26.4 us -> 6.39 us
    convert_element_type x3 -> x0, local copies, waits for them, and re-layouts: 12.6 us -> none  [the longest x2 8.81 us: shards(): residual = gathered[:, :, :columns].reshape([sections, expert_groups] + [...]
    dot_general x1 -> x0, matrix products: 11.8 us -> none  [shards(): jnp.dot(normed, expert_in[0].reshape(width, 2 * slice_width), preferred_e...]
    convert_element_type x2 -> x0, other arithmetic: 9 us -> none  [the longest x1 6.36 us: shards(): normed = (residual * lax.rsqrt(jnp.mean(residual * residual, axis=1, keep...]
    dot_general x1, matrix products: 8.61 us -> 3.34 us  [shards(): jnp.dot(activated, expert_out[0], preferred_element_type=jnp.float32)]
    reduce_sum x1 -> x0, other arithmetic: 4.68 us -> none  [shards(): jnp.mean(residual * residual, axis=1, keepdims=True) + 1e-06]
    pallas_call x2, Pallas kernels: 39.7 us -> 37.6 us  [gather(): pl.pallas_call(functools.partial(gather_kernel, orders, spans, flat), out...]
  transfers between devices with their start and end apart: 1 -> 1, of which waited for: 0 -> 0; matrix products, arithmetic and copies ran while one was open for 22% -> 13% of each run, Pallas kernels for 16% -> 19%
where the time goes in v3:
time: 138 us
  Pallas kernels  98.6 us (71%)
  local copies, waits for them, and re-layouts  13.7 us (10%)
  matrix products  13.7 us (10%)
  starting transfers between devices  7.39 us (5%)
  other arithmetic  3.57 us (3%)
    pallas_call x2, Pallas kernels, gather(): pl.pallas_call(functools.partial(gather_kernel, orders, spans, flat), out...  37.6 us
    pallas_call x1, Pallas kernels, reduce_rows(): pl.pallas_call(functools.partial(reduce_kernel, core, halving, whole_bits...  28 us
    pallas_call x1, Pallas kernels, hidden_units(): pl.pallas_call(functools.partial(hidden_kernel, deep), out_shape=jax.Shap...  24.7 us
    all_to_all x1, starting transfers between devices, shards(): lax.all_to_all(unit_hidden, 'grp', split_axis=1, concat_axis=0, tiled=True)  7.39 us
    dot_general x1, matrix products, shards(): jnp.einsum('bhc,hcv->bhv', latent_out, w_uv[:, 0], preferred_element_type...  7.07 us
    pallas_call x1, Pallas kernels, project(): pl.pallas_call(functools.partial(project_kernel, heads_step), grid=(heads...  7.05 us
    unnamed x19, local copies, waits for them, and re-layouts  6.39 us
    reshape x2, local copies, waits for them, and re-layouts, shards(): group_blocks.reshape(expert_groups, parts, unit, -1).transpose(0, 2, 1, 3)  5.26 us
  transfers between devices with their start and end apart: 1, of which 0 were waited for; matrix products, arithmetic and copies ran while one was open for 13% of the time, Pallas kernels for 19%

profile of v3, /device:TPU:0, one launch (start us, length us, event | category | flops | bytes accessed | tf_op | source)
XLA Modules:
  0.0 138.0 jit_solution(16935846465955872041)
XLA Ops:
  0.0 1.0 all_to_all.10
  1.0 0.7 copy.22
  1.7 7.4 %all-to-all-start = ((bf16[4,16,448]{2,0,1:T(4,128)(2,1)}), bf16[4,16,448]{2,0,1:T(4,128)(2,1)S(1)}, u32[]{:S(2)}, u32[]{:S(2)}) async-start(bf16[4,16,448]{2,0,1:T(4,128)(2,1)} %copy.22), calls=%async_computation | async-start | bytes 131072 | tf_op jit(solution)/shard_map/all_to_all | solution.py:431
  9.8 0.7 iota_compare_fusion.1
  10.6 0.8 fusion.25
  11.4 1.2 fusion.15
  12.7 1.3 convolution_convert_fusion
  14.0 7.1 %fusion.12 = bf16[128,4,128]{2,1,0:T(4,128)(2,1)S(1)} fusion(bf16[128,1,512,128]{3,2,1,0:T(8,128)(2,1)} %param.16, bf16[4,128,512]{2,1,0:T(8,128)(2,1)S(1)} %convolution_convert_fusion), kind=kOutput, calls=%fused_computation.9 | convolution fusion | flops 67174400 | bytes 17432576 | tf_op jit(solution)/shard_map/bhc,hcv->bhv/dot_general | solution.py:450
  21.1 19.5 %gather_heads.1 = bf16[16,32,2048]{2,1,0:T(8,128)(2,1)S(1)} custom-call(bf16[32,2048]{1,0:T(8,128)(2,1)S(1)} %reshape.71.x_ref), custom_call_target="tpu_custom_call" | custom-call | tf_op jit(solution)/shard_map/gather_heads/pallas_call | solution.py:142
  40.7 2.2 %reshape.72 = bf16[16,8,4,2048]{3,2,1,0:T(4,128)(2,1)} reshape(bf16[16,32,2048]{2,1,0:T(8,128)(2,1)S(1)} %gather_heads.1) | data formatting | bytes 4194304 | tf_op jit(solution)/shard_map/reshape | solution.py:463
  42.9 3.0 %copy.21 = bf16[16,8,4,2048]{3,1,2,0:T(8,128)(2,1)S(1)} copy(bf16[16,8,4,2048]{3,2,1,0:T(4,128)(2,1)} %reshape.72) | data formatting | bytes 4194304 | tf_op jit(solution)/shard_map/reshape | solution.py:463
  46.0 1.2 copy.25
  47.2 5.2 %copy-done.2 = bf16[128,1,128,448]{2,3,1,0:T(8,128)(2,1)S(1)} copy-done((bf16[128,1,128,448]{2,3,1,0:T(8,128)(2,1)S(1)}, bf16[128,1,128,448]{2,3,1,0:T(8,128)(2,1)}, u32[]{:S(2)}) %copy-start.2) | copy-done | bytes 14680088
  52.3 7.0 %project.1 = f32[64,448]{1,0:T(8,128)S(1)} custom-call(bf16[64,16384]{1,0:T(8,128)(2,1)S(1)} %bitcast.50, bf16[128,448,128]{2,1,0:T(8,128)(2,1)S(1)} %bitcast.49), custom_call_target="tpu_custom_call" | custom-call | flops 939524096 | bytes 16777216 | tf_op jit(solution)/shard_map/project/pallas_call | solution.py:47
  59.6 18.1 %gather_columns.1.x_ref = bf16[32,64,480]{2,1,0:T(8,128)(2,1)S(1)} custom-call(bf16[64,480]{1,0:T(8,128)(2,1)S(1)} %pad_maximum_fusion.x_ref), custom_call_target="tpu_custom_call" | custom-call | tf_op jit(solution)/shard_map/gather_columns/pallas_call | solution.py:142
  77.7 0.1 slice.7
  77.8 0.1 bitcast_reduce_fusion
  77.9 0.1 gt.16
  78.1 1.3 norm_rows.1
  79.4 24.7 %hidden_units.1 = bf16[128,1024]{1,0:T(8,128)(2,1)S(1)} custom-call(bf16[128,7168]{1,0:T(8,128)(2,1)S(1)} %get-tuple-element.8.x_ref, bf16[7168,8,2,128]{3,2,1,0:T(2,128)(2,1)} %bitcast.52), custom_call_target="tpu_custom_call" | custom-call | tf_op jit(solution)/shard_map/hidden_units/pallas_call | solution.py:382
  104.2 0.7 fusion.28
  105.1 3.3 %fusion.8 = bf16[128,7168]{1,0:T(8,128)(2,1)} fusion(bf16[128,1024]{1,0:T(8,128)(2,1)S(1)} %hidden_units.1, bf16[1,1024,7168]{2,1,0:T(8,128)(2,1)S(1)} %bitcast.54, f32[128]{0:T(128)S(1)} %select_reduce_fusion), kind=kOutput, calls=%fused_computation.6 | convolution fusion | flops 1880883200 | bytes 16777728 | tf_op jit(solution)/shard_map/dot_general | solution.py:505
  108.4 28.0 %reduce_rows.1 = bf16[16,7168]{1,0:T(8,128)(2,1)} custom-call(bf16[8,16,7168]{2,1,0:T(8,128)(2,1)} %bitcast.56), custom_call_target="tpu_custom_call" | custom-call | tf_op jit(solution)/shard_map/reduce_rows/pallas_call | solution.py:255
  136.4 1.6 %add_convert_fusion.1 = bf16[4,7168]{1,0:T(4,128)(2,1)} fusion(bf16[16,7168]{1,0:T(8,128)(2,1)} %reduce_rows.1, s32[]{:T(128)S(6)} %select_n.69, bf16[128,7168]{1,0:T(8,128)(2,1)S(1)} %get-tuple-element.7, s32[]{:T(128)S(6)} %select_n.66), kind=kLoop, calls=%fused_computation.24 | loop fusion | flops 114688 | bytes 172040 | tf_op jit(solution)/shard_map/convert_element_type | solution.py:524
  (34 shorter events, 0.6 us)
Async XLA Ops:
  0.0 11.4 %copy-start = (bf16[4,128,1,576]{1,3,2,0:T(8,128)(2,1)S(1)}, bf16[4,128,1,576]{1,3,2,0:T(8,128)(2,1)}, u32[]{:S(2)}) copy-start(bf16[4,128,1,576]{1,3,2,0:T(8,128)(2,1)} %param.13) | copy-start | bytes 1769476
  1.7 57.7 %all-to-all-start = ((bf16[4,16,448]{2,0,1:T(4,128)(2,1)}), bf16[4,16,448]{2,0,1:T(4,128)(2,1)S(1)}, u32[]{:S(2)}, u32[]{:S(2)}) async-start(bf16[4,16,448]{2,0,1:T(4,128)(2,1)} %copy.22), calls=%async_computation | async-start | bytes 131072 | tf_op jit(solution)/shard_map/all_to_all | solution.py:431
  47.2 5.2 %copy-start.2 = (bf16[128,1,128,448]{2,3,1,0:T(8,128)(2,1)S(1)}, bf16[128,1,128,448]{2,3,1,0:T(8,128)(2,1)}, u32[]{:S(2)}) copy-start(bf16[128,1,128,448]{2,3,1,0:T(8,128)(2,1)} %param.17) | copy-start | bytes 44040196
  52.3 25.7 %copy-start.3 = (f32[7168]{0:T(1024)S(1)}, f32[7168]{0:T(1024)}, u32[]{:S(2)}) copy-start(f32[7168]{0:T(1024)} %param.18) | copy-start | bytes 86020
  78.1 26.9 %slice-start = ((s8[14680064]{0:T(1024)(128)(4,1)}), s8[4194304]{0:T(1024)(128)(4,1)S(1)}, s32[]{:S(2)}) async-start(s8[14680064]{0:T(1024)(128)(4,1)} %bitcast.53), calls=%async_computation.1 | async-start | bytes 8388608
  79.4 24.8 %copy-start.4 = (bf16[7168,32]{0,1:T(8,128)(2,1)S(1)}, bf16[7168,32]{0,1:T(8,128)(2,1)}, u32[]{:S(2)}) copy-start(bf16[7168,32]{0,1:T(8,128)(2,1)} %param.19) | copy-start | bytes 1376260
  79.4 25.6 %slice-start.1 = ((s8[14680064]{0:T(1024)(128)(4,1)}), s8[4194304]{0:T(1024)(128)(4,1)S(1)}, s32[]{:S(2)}) async-start(s8[14680064]{0:T(1024)(128)(4,1)} %bitcast.53), calls=%async_computation.2 | async-start | bytes 8388608
  79.4 25.6 %slice-start.2 = ((s8[14680064]{0:T(1024)(128)(4,1)}), s8[4194304]{0:T(1024)(128)(4,1)S(1)}, s32[]{:S(2)}) async-start(s8[14680064]{0:T(1024)(128)(4,1)} %bitcast.53), calls=%async_computation.3 | async-start | bytes 8388608
  79.4 25.6 %slice-start.3 = ((s8[14680064]{0:T(1024)(128)(4,1)}), s8[2097152]{0:T(1024)(128)(4,1)S(1)}, s32[]{:S(2)}) async-start(s8[14680064]{0:T(1024)(128)(4,1)} %bitcast.53), calls=%async_computation.4 | async-start | bytes 4194304
  105.0 32.9 %copy-start.1 = (bf16[4,128,1,576]{1,3,2,0:T(8,128)(2,1)S(1)}, bf16[4,128,1,576]{1,3,2,0:T(8,128)(2,1)}, u32[]{:S(2)}) copy-start(bf16[4,128,1,576]{1,3,2,0:T(8,128)(2,1)} %param.13) | copy-start | bytes 1769476

commit v4 on v3

--- a/solution.py
+++ b/solution.py
@@ -54,7 +54,7 @@
         out_specs=pl.BlockSpec((tokens, columns), lambda i: (0, 0)),
         out_shape=jax.ShapeDtypeStruct((tokens, columns), jnp.float32),
         scratch_shapes=[pltpu.VMEM((tokens, columns), jnp.float32)],
-        compiler_params=pltpu.CompilerParams(vmem_limit_bytes=16 * 1024 * 1024),
+        compiler_params=pltpu.CompilerParams(vmem_limit_bytes=56 * 1024 * 1024),
         cost_estimate=pl.CostEstimate(
             flops=2 * tokens * heads * value_width * columns,
             bytes_accessed=2 * heads * value_width * (columns + tokens),
@@ -376,7 +376,7 @@
 def hidden_units(rows, weight):
     depth, _, slice_width = weight.shape
     tokens = rows.shape[0]
-    deep, slots = 256, 3
+    deep, slots = 256, 8
     tiles = slice_width // 128
     lanes = weight.reshape(depth, 2, tiles, 128).transpose(0, 2, 1, 3)
     return pl.pallas_call(

time: 138 us -> 143 us (1.036)
  Pallas kernels: 98.6 us -> 106 us
  local copies, waits for them, and re-layouts: 13.7 us -> 9.85 us
    pallas_call x1, Pallas kernels: 7.05 us -> 14.8 us  [project(): pl.pallas_call(functools.partial(project_kernel, heads_step), grid=(heads...]
    unnamed x19 -> x17, local copies, waits for them, and re-layouts: 6.39 us -> 2.58 us
  transfers between devices with their start and end apart: 1 -> 1, of which waited for: 0 -> 0; matrix products, arithmetic and copies ran while one was open for 13% -> 13% of each run, Pallas kernels for 19% -> 24%
where the time goes in v4:
time: 143 us
  Pallas kernels  106 us (74%)
  matrix products  13.7 us (10%)
  local copies, waits for them, and re-layouts  9.85 us (7%)
  starting transfers between devices  7.39 us (5%)
  other arithmetic  4.48 us (3%)
    pallas_call x2, Pallas kernels, gather(): pl.pallas_call(functools.partial(gather_kernel, orders, spans, flat), out...  37.5 us
    pallas_call x1, Pallas kernels, reduce_rows(): pl.pallas_call(functools.partial(reduce_kernel, core, halving, whole_bits...  28.1 us
    pallas_call x1, Pallas kernels, hidden_units(): pl.pallas_call(functools.partial(hidden_kernel, deep), out_shape=jax.Shap...  24.6 us
    pallas_call x1, Pallas kernels, project(): pl.pallas_call(functools.partial(project_kernel, heads_step), grid=(heads...  14.8 us
    all_to_all x1, starting transfers between devices, shards(): lax.all_to_all(unit_hidden, 'grp', split_axis=1, concat_axis=0, tiled=True)  7.39 us
    dot_general x1, matrix products, shards(): jnp.einsum('bhc,hcv->bhv', latent_out, w_uv[:, 0], preferred_element_type...  7.07 us
    reshape x2, local copies, waits for them, and re-layouts, shards(): group_blocks.reshape(expert_groups, parts, unit, -1).transpose(0, 2, 1, 3)  5.26 us
    dot_general x1, matrix products, shards(): jnp.dot(activated, expert_out[0], preferred_element_type=jnp.float32)  3.34 us
  transfers between devices with their start and end apart: 1, of which 0 were waited for; matrix products, arithmetic and copies ran while one was open for 13% of the time, Pallas kernels for 24%

profile of v4, /device:TPU:0, one launch (start us, length us, event | category | flops | bytes accessed | tf_op | source)
XLA Modules:
  0.0 142.8 jit_solution(360380389435362400)
XLA Ops:
  0.0 1.0 all_to_all.10
  1.0 0.7 copy.22
  1.7 7.4 %all-to-all-start = ((bf16[4,16,448]{2,0,1:T(4,128)(2,1)}), bf16[4,16,448]{2,0,1:T(4,128)(2,1)S(1)}, u32[]{:S(2)}, u32[]{:S(2)}) async-start(bf16[4,16,448]{2,0,1:T(4,128)(2,1)} %copy.22), calls=%async_computation | async-start | bytes 131072 | tf_op jit(solution)/shard_map/all_to_all | solution.py:431
  9.8 0.7 iota_compare_fusion.1
  10.6 0.8 fusion.25
  11.4 1.2 fusion.15
  12.7 1.3 convolution_convert_fusion
  14.0 7.1 %fusion.12 = bf16[128,4,128]{2,1,0:T(4,128)(2,1)S(1)} fusion(bf16[128,1,512,128]{3,2,1,0:T(8,128)(2,1)} %param.16, bf16[4,128,512]{2,1,0:T(8,128)(2,1)S(1)} %convolution_convert_fusion), kind=kOutput, calls=%fused_computation.9 | convolution fusion | flops 67174400 | bytes 17432576 | tf_op jit(solution)/shard_map/bhc,hcv->bhv/dot_general | solution.py:450
  21.1 19.5 %gather_heads.1 = bf16[16,32,2048]{2,1,0:T(8,128)(2,1)S(1)} custom-call(bf16[32,2048]{1,0:T(8,128)(2,1)S(1)} %reshape.71.x_ref), custom_call_target="tpu_custom_call" | custom-call | tf_op jit(solution)/shard_map/gather_heads/pallas_call | solution.py:142
  40.7 2.2 %reshape.72 = bf16[16,8,4,2048]{3,2,1,0:T(4,128)(2,1)} reshape(bf16[16,32,2048]{2,1,0:T(8,128)(2,1)S(1)} %gather_heads.1) | data formatting | bytes 4194304 | tf_op jit(solution)/shard_map/reshape | solution.py:463
  42.9 3.0 %copy.21 = bf16[16,8,4,2048]{3,1,2,0:T(8,128)(2,1)S(1)} copy(bf16[16,8,4,2048]{3,2,1,0:T(4,128)(2,1)} %reshape.72) | data formatting | bytes 4194304 | tf_op jit(solution)/shard_map/reshape | solution.py:463
  45.9 2.5 %copy.25 = bf16[8,8,8,2048]{3,1,2,0:T(8,128)(2,1)} copy(bf16[8,8,8,2048]{3,2,1,0:T(8,128)(2,1)S(1)} %bitcast.54) | data formatting | bytes 4194304
  48.5 14.8 %project.1 = f32[64,448]{1,0:T(8,128)} custom-call(bf16[64,16384]{1,0:T(8,128)(2,1)} %bitcast.55, bf16[128,448,128]{2,1,0:T(8,128)(2,1)} %bitcast.53), custom_call_target="tpu_custom_call" | custom-call | flops 939524096 | bytes 16777216 | tf_op jit(solution)/shard_map/project/pallas_call | solution.py:47
  63.4 0.9 add_convert_fusion
  64.4 18.0 %gather_columns.1.x_ref = bf16[32,64,480]{2,1,0:T(8,128)(2,1)S(1)} custom-call(bf16[64,480]{1,0:T(8,128)(2,1)S(1)} %pad_maximum_fusion.x_ref), custom_call_target="tpu_custom_call" | custom-call | tf_op jit(solution)/shard_map/gather_columns/pallas_call | solution.py:142
  82.4 0.1 slice.7
  82.5 0.1 bitcast_reduce_fusion
  82.7 0.1 gt.16
  82.8 1.3 norm_rows.1
  84.2 24.6 %hidden_units.1 = bf16[128,1024]{1,0:T(8,128)(2,1)S(1)} custom-call(bf16[128,7168]{1,0:T(8,128)(2,1)S(1)} %get-tuple-element.8.x_ref, bf16[7168,8,2,128]{3,2,1,0:T(2,128)(2,1)} %bitcast.50), custom_call_target="tpu_custom_call" | custom-call | tf_op jit(solution)/shard_map/hidden_units/pallas_call | solution.py:382
  108.8 0.7 fusion.28
  109.7 3.3 %fusion.8 = bf16[128,7168]{1,0:T(8,128)(2,1)} fusion(bf16[128,1024]{1,0:T(8,128)(2,1)S(1)} %hidden_units.1, bf16[1,1024,7168]{2,1,0:T(8,128)(2,1)S(1)} %bitcast.52, f32[128]{0:T(128)S(1)} %select_reduce_fusion), kind=kOutput, calls=%fused_computation.6 | convolution fusion | flops 1880883200 | bytes 16777728 | tf_op jit(solution)/shard_map/dot_general | solution.py:505
  113.1 28.1 %reduce_rows.1 = bf16[16,7168]{1,0:T(8,128)(2,1)} custom-call(bf16[8,16,7168]{2,1,0:T(8,128)(2,1)} %bitcast.56), custom_call_target="tpu_custom_call" | custom-call | tf_op jit(solution)/shard_map/reduce_rows/pallas_call | solution.py:255
  141.2 1.6 %add_convert_fusion.1 = bf16[4,7168]{1,0:T(4,128)(2,1)} fusion(bf16[16,7168]{1,0:T(8,128)(2,1)} %reduce_rows.1, s32[]{:T(128)S(6)} %select_n.69, bf16[128,7168]{1,0:T(8,128)(2,1)S(1)} %get-tuple-element.7, s32[]{:T(128)S(6)} %select_n.66), kind=kLoop, calls=%fused_computation.24 | loop fusion | flops 114688 | bytes 172040 | tf_op jit(solution)/shard_map/convert_element_type | solution.py:524
  (32 shorter events, 0.6 us)
Async XLA Ops:
  0.0 11.4 %copy-start = (bf16[4,128,1,576]{1,3,2,0:T(8,128)(2,1)S(1)}, bf16[4,128,1,576]{1,3,2,0:T(8,128)(2,1)}, u32[]{:S(2)}) copy-start(bf16[4,128,1,576]{1,3,2,0:T(8,128)(2,1)} %param.13) | copy-start | bytes 1769476
  1.7 61.7 %all-to-all-start = ((bf16[4,16,448]{2,0,1:T(4,128)(2,1)}), bf16[4,16,448]{2,0,1:T(4,128)(2,1)S(1)}, u32[]{:S(2)}, u32[]{:S(2)}) async-start(bf16[4,16,448]{2,0,1:T(4,128)(2,1)} %copy.22), calls=%async_computation | async-start | bytes 131072 | tf_op jit(solution)/shard_map/all_to_all | solution.py:431
  48.5 34.4 %copy-start.2 = (f32[7168]{0:T(1024)S(1)}, f32[7168]{0:T(1024)}, u32[]{:S(2)}) copy-start(f32[7168]{0:T(1024)} %param.18) | copy-start | bytes 86020
  82.8 26.8 %slice-start = ((s8[14680064]{0:T(1024)(128)(4,1)}), s8[4194304]{0:T(1024)(128)(4,1)S(1)}, s32[]{:S(2)}) async-start(s8[14680064]{0:T(1024)(128)(4,1)} %bitcast.51), calls=%async_computation.1 | async-start | bytes 8388608
  84.1 24.7 %copy-start.3 = (bf16[7168,32]{0,1:T(8,128)(2,1)S(1)}, bf16[7168,32]{0,1:T(8,128)(2,1)}, u32[]{:S(2)}) copy-start(bf16[7168,32]{0,1:T(8,128)(2,1)} %param.19) | copy-start | bytes 1376260
  84.2 25.5 %slice-start.1 = ((s8[14680064]{0:T(1024)(128)(4,1)}), s8[4194304]{0:T(1024)(128)(4,1)S(1)}, s32[]{:S(2)}) async-start(s8[14680064]{0:T(1024)(128)(4,1)} %bitcast.51), calls=%async_computation.2 | async-start | bytes 8388608
  84.2 25.5 %slice-start.2 = ((s8[14680064]{0:T(1024)(128)(4,1)}), s8[4194304]{0:T(1024)(128)(4,1)S(1)}, s32[]{:S(2)}) async-start(s8[14680064]{0:T(1024)(128)(4,1)} %bitcast.51), calls=%async_computation.3 | async-start | bytes 8388608
  84.2 25.5 %slice-start.3 = ((s8[14680064]{0:T(1024)(128)(4,1)}), s8[2097152]{0:T(1024)(128)(4,1)S(1)}, s32[]{:S(2)}) async-start(s8[14680064]{0:T(1024)(128)(4,1)} %bitcast.51), calls=%async_computation.4 | async-start | bytes 4194304
  109.7 33.1 %copy-start.1 = (bf16[4,128,1,576]{1,3,2,0:T(8,128)(2,1)S(1)}, bf16[4,128,1,576]{1,3,2,0:T(8,128)(2,1)}, u32[]{:S(2)}) copy-start(bf16[4,128,1,576]{1,3,2,0:T(8,128)(2,1)} %param.13) | copy-start | bytes 1769476
